TPU v7x, 32 devices: a whole 2x2x4 slice. The times are simulated.
32 devices in a mesh: sample: 8 (over z, y), space: 4 (over x, core).
Axes of the slice: x: 2, y: 2, z: 4, core: 2. Of those that a mesh axis runs over, the one named last changes fastest.
Arguments:
- volumes: bfloat16 [8, 32, 64, 1024], P('sample', None, 'space'), may hold values from -6 to 6
- first_weight: bfloat16 [64, 864], replicated, may hold values from -0.21875 to 0.21875
- first_bias: float32 [64], replicated, may hold values from -3 to 3
- second_weight: bfloat16 [128, 1728], replicated, may hold values from -0.15625 to 0.15625
- second_bias: float32 [128], replicated, may hold values from -3 to 3
- cotangent: bfloat16 [8, 128, 32, 256], P('sample', None, 'space'), may hold values from -6 to 6
Outputs:
- activation: bfloat16 [8, 128, 32, 256], P('sample', None, 'space')
- input_grad: bfloat16 [8, 32, 64, 1024], P('sample', None, 'space')
- first_wgrad: float32 [64, 864], replicated
- first_bgrad: float32 [64], replicated
- second_wgrad: float32 [128, 1728], replicated
- second_bgrad: float32 [128], replicated
All inputs are finite; a program needn't handle non-finite values.
Results may differ from a plain program's by a relative error of at most 0.013.
Values may be sent and summed in bfloat16 or wider, within the bound.
A program may use at most 128 MiB of HBM per device.

v0:
```python
import functools
import math

import jax
import jax.numpy as jnp
import numpy as np
from jax import lax
from jax.experimental import pallas as pl
from jax.experimental.pallas import tpu as pltpu
from jax.sharding import PartitionSpec as P

CH_IN = 32
CH_MID = 64
CH_OUT = 128
VOL_HEIGHT = 64
VOL_WIDTH = 16

VMEM_BYTES = 56 * 1024 * 1024
BF = jnp.bfloat16
F32 = jnp.float32


def tap_masks(height, width):
    rows = np.arange(height * width) // width
    cols = np.arange(height * width) % width
    out = []
    for tap in range(9):
        up, side = tap // 3 - 1, tap % 3 - 1
        good = (rows + up >= 0) & (rows + up < height) & (cols + side >= 0) & (cols + side < width)
        out.append(np.repeat(good[None], 16, 0))
    return jnp.asarray(np.concatenate(out).astype(np.float32), BF)


def pool_matrix():
    cell = np.arange(32 * VOL_WIDTH)
    target = (cell // VOL_WIDTH // 2) * (VOL_WIDTH // 2) + cell % VOL_WIDTH // 2
    return (target[:, None] == np.arange(128)[None]).astype(np.float32) * 0.125


def banded(weight, planes):
    taps = weight.shape[1] // 3
    return jnp.concatenate(
        [jnp.pad(weight, ((0, 0), (j * taps, (planes - 1 - j) * taps))) for j in range(planes)]
    )


def turned(weight, channels):
    outs = weight.shape[0]
    return weight.reshape(outs, 27, channels)[:, ::-1].transpose(2, 1, 0).reshape(channels, 27 * outs)


def put_columns(x, base, col, mask, width):
    channels, cells = x.shape
    for tap in range(9):
        by = (tap // 3 - 1) * width + tap % 3 - 1
        moved = x
        if by:
            good = mask[tap * 16 : (tap + 1) * 16, :]
            moved = pltpu.roll(x, (-by) % cells, 1) * jnp.concatenate([good] * (channels // 16), 0)
        start = pl.multiple_of(base + tap * channels, 16)
        col[pl.ds(start, channels), :] = moved


def fill_columns(before, x, after, col, mask, channels, width):
    planes = x.shape[0] // channels
    put_columns(before[...], 0, col, mask, width)
    put_columns(after[...], (planes + 1) * 9 * channels, col, mask, width)

    def body(p, carry):
        start = pl.multiple_of(p * channels, channels)
        put_columns(x[pl.ds(start, channels), :], (p + 1) * (9 * channels), col, mask, width)
        return carry

    lax.fori_loop(0, planes, body, 0)


def sigmoid(v):
    return 0.5 * jnp.tanh(0.5 * v) + 0.5


def first_kernel(before, x, after, weight, bias, mask, pool, pooled, slope, col):
    fill_columns(before, x, after, col, mask, CH_IN, VOL_WIDTH)
    group = weight.shape[0] // CH_MID
    taps = 9 * CH_IN
    chunks = x.shape[1] // 512

    def body(step, carry):
        i, n = step // chunks, step % chunks
        lanes = pl.ds(pl.multiple_of(n * 512, 512), 512)
        window = col[pl.ds(pl.multiple_of(i * (group * taps), 16), (group + 2) * taps), lanes]
        pre = jnp.dot(weight[...], window, preferred_element_type=F32) + bias[...]
        s = sigmoid(pre)
        act = pre * s
        rows = pl.ds(pl.multiple_of(i * (group * CH_MID), 64), group * CH_MID)
        slope[rows, lanes] = (s + act * (1.0 - s)).astype(BF)
        sums = jnp.concatenate(
            [
                act[2 * j * CH_MID : (2 * j + 1) * CH_MID] + act[(2 * j + 1) * CH_MID : (2 * j + 2) * CH_MID]
                for j in range(group // 2)
            ]
        ).astype(BF)
        half = pl.ds(pl.multiple_of(i * (group // 2 * CH_MID), 64), group // 2 * CH_MID)
        small = pl.ds(pl.multiple_of(n * 128, 128), 128)
        pooled[half, small] = jnp.dot(sums, pool[...], preferred_element_type=F32).astype(BF)
        return carry

    lax.fori_loop(0, x.shape[0] // (group * CH_IN) * chunks, body, 0)


def second_kernel(before, x, after, weight, bias, cot, mask, act_out, grad_out, col):
    fill_columns(before, x, after, col, mask, CH_MID, VOL_WIDTH // 2)
    group = weight.shape[0] // CH_OUT
    taps = 9 * CH_MID

    def body(i, carry):
        window = col[pl.ds(pl.multiple_of(i * (group * taps), 16), (group + 2) * taps), :]
        pre = jnp.dot(weight[...], window, preferred_element_type=F32) + bias[...]
        s = sigmoid(pre)
        act = pre * s
        rows = pl.ds(pl.multiple_of(i * (group * CH_OUT), 128), group * CH_OUT)
        act_out[rows, :] = act.astype(BF)
        grad_out[rows, :] = (cot[rows, :].astype(F32) * (s + act * (1.0 - s))).astype(BF)
        return carry

    lax.fori_loop(0, x.shape[0] // (group * CH_MID), body, 0)


def weight_kernel(outs, grad, col, total, wide):
    cells = grad.shape[1]
    planes = grad.shape[0] // outs
    taps = col.shape[0] // (planes + 2)
    edge = jnp.zeros((2 * outs, cells), BF)
    wide[0 : 2 * outs, :] = edge
    wide[(planes + 2) * outs : (planes + 4) * outs, :] = edge
    wide[2 * outs : (planes + 2) * outs, :] = grad[...]
    total[...] = jnp.zeros_like(total)
    ones = jnp.ones((16, cells), BF)

    def body(p, carry):
        left = jnp.concatenate([col[pl.ds(pl.multiple_of(p * taps, 16), taps), :], ones])
        right = wide[pl.ds(pl.multiple_of(p * outs, 64), 3 * outs), :]
        total[...] += lax.dot_general(
            left, right, (((1,), (1,)), ((), ())), preferred_element_type=F32
        )
        return carry

    lax.fori_loop(0, planes + 2, body, 0)


def spread_kernel(before, x, after, weight, mask, spread, slope, grad_out, col):
    fill_columns(before, x, after, col, mask, CH_OUT, VOL_WIDTH // 2)
    group = weight.shape[0] // CH_MID
    taps = 9 * CH_OUT

    def body(i, carry):
        window = col[pl.ds(pl.multiple_of(i * (group * taps), 16), (group + 2) * taps), :]
        pooled_grad = jnp.dot(weight[...], window, preferred_element_type=F32).astype(BF)
        for n in range(x.shape[1] // 128):
            big = jnp.dot(
                pooled_grad[:, n * 128 : (n + 1) * 128], spread[...], preferred_element_type=F32
            )
            for j in range(2 * group):
                rows = pl.ds(pl.multiple_of(i * (2 * group * CH_MID) + j * CH_MID, 64), CH_MID)
                lanes = slice(n * 512, (n + 1) * 512)
                part = big[j // 2 * CH_MID : (j // 2 + 1) * CH_MID]
                grad_out[rows, lanes] = (part * slope[rows, lanes].astype(F32)).astype(BF)
        return carry

    lax.fori_loop(0, x.shape[0] // (group * CH_OUT), body, 0)


def input_kernel(before, x, after, weight, mask, out, col):
    fill_columns(before, x, after, col, mask, CH_MID, VOL_WIDTH)
    group = weight.shape[0] // CH_IN
    taps = 9 * CH_MID
    chunks = x.shape[1] // 256

    def body(step, carry):
        i, n = step // chunks, step % chunks
        lanes = pl.ds(pl.multiple_of(n * 256, 256), 256)
        window = col[pl.ds(pl.multiple_of(i * (group * taps), 16), (group + 2) * taps), lanes]
        rows = pl.ds(pl.multiple_of(i * (group * CH_IN), 32), group * CH_IN)
        out[rows, lanes] = jnp.dot(weight[...], window, preferred_element_type=F32).astype(BF)
        return carry

    lax.fori_loop(0, x.shape[0] // (group * CH_MID) * chunks, body, 0)


def call(kernel, outs, scratch, flops, *operands):
    whole = pl.BlockSpec(memory_space=pltpu.VMEM)
    moved = sum(o.size * o.dtype.itemsize for o in operands)
    return pl.pallas_call(
        kernel,
        out_shape=[jax.ShapeDtypeStruct(shape, dtype) for shape, dtype in outs],
        in_specs=[whole] * len(operands),
        out_specs=[whole] * len(outs),
        scratch_shapes=[pltpu.VMEM(shape, dtype) for shape, dtype in scratch],
        compiler_params=pltpu.CompilerParams(vmem_limit_bytes=VMEM_BYTES),
        cost_estimate=pl.CostEstimate(flops=flops, bytes_accessed=moved, transcendentals=0),
    )(*operands)


def halo(x, rows):
    size = lax.axis_size("space")
    up = [(i, i + 1) for i in range(size - 1)]
    down = [(j, i) for i, j in up]
    before = lax.ppermute(x[x.shape[0] - rows :], "space", up)
    after = lax.ppermute(x[:rows], "space", down)
    return before, after


def group_of(planes, most):
    group = most
    while planes % group:
        group //= 2
    return group


def one_sample(volume, cot, weights, masks, pools):
    planes, cells = volume.shape[1:]
    half, small = planes // 2, cells // 4
    first_w, first_b, second_w, second_b, spread_w, input_w = weights
    big_mask, small_mask = masks
    x = volume.transpose(1, 0, 2).reshape(planes * CH_IN, cells)
    cot = cot.transpose(1, 0, 2).reshape(half * CH_OUT, small)

    work = 2 * planes * cells * 27 * CH_IN * CH_MID
    before, after = halo(x, CH_IN)
    pooled, slope, col = call(
        first_kernel,
        [
            ((half * CH_MID, small), BF),
            ((planes * CH_MID, cells), BF),
            (((planes + 2) * 9 * CH_IN, cells), BF),
        ],
        [],
        4 * work,
        before, x, after, first_w, first_b, big_mask, pools[0],
    )
    before, after = halo(pooled, CH_MID)
    act, grad, small_col = call(
        second_kernel,
        [
            ((half * CH_OUT, small), BF),
            ((half * CH_OUT, small), BF),
            (((half + 2) * 9 * CH_MID, small), BF),
        ],
        [],
        work,
        before, pooled, after, second_w, second_b, cot, small_mask,
    )
    before, after = halo(grad, CH_OUT)
    (second_total,) = call(
        functools.partial(weight_kernel, CH_OUT),
        [((9 * CH_MID + 16, 3 * CH_OUT), F32)],
        [(((half + 4) * CH_OUT, small), BF)],
        2 * work,
        grad, small_col,
    )
    (first_grad,) = call(
        spread_kernel,
        [((planes * CH_MID, cells), BF)],
        [(((half + 2) * 9 * CH_OUT, small), BF)],
        2 * work,
        before, grad, after, spread_w, small_mask, pools[1], slope,
    )
    before, after = halo(first_grad, CH_MID)
    (first_total,) = call(
        functools.partial(weight_kernel, CH_MID),
        [((9 * CH_IN + 16, 3 * CH_MID), F32)],
        [(((planes + 4) * CH_MID, cells), BF)],
        4 * work,
        first_grad, col,
    )
    (input_grad,) = call(
        input_kernel,
        [((planes * CH_IN, cells), BF)],
        [(((planes + 2) * 9 * CH_MID, cells), BF)],
        6 * work,
        before, first_grad, after, input_w, big_mask,
    )
    act = act.reshape(half, CH_OUT, small).transpose(1, 0, 2)
    input_grad = input_grad.reshape(planes, CH_IN, cells).transpose(1, 0, 2)
    return act, input_grad, first_total, second_total


def unpacked(total, outs):
    taps = total.shape[0] - 16
    wgrad = total[:taps].reshape(taps, 3, outs)[:, ::-1].transpose(2, 1, 0).reshape(outs, 3 * taps)
    return wgrad, total[taps, :outs]


def per_device(volumes, first_weight, first_bias, second_weight, second_bias, cotangent):
    samples, _, planes, cells = volumes.shape
    all_samples = samples * lax.axis_size("sample")
    scale = 1.0 / math.sqrt(all_samples * planes * lax.axis_size("space") * cells / 8.0)
    half = planes // 2
    g1, g2 = group_of(planes, 4), group_of(half, 2)
    g3, g4 = group_of(half, 4), group_of(planes, 4)
    weights = (
        banded(first_weight, g1),
        jnp.tile(first_bias, g1).reshape(-1, 1),
        banded(second_weight, g2),
        jnp.tile(second_bias, g2).reshape(-1, 1),
        banded(turned(second_weight, CH_MID), g3),
        banded(turned(first_weight, CH_IN), g4),
    )
    masks = (tap_masks(VOL_HEIGHT, VOL_WIDTH), tap_masks(VOL_HEIGHT // 2, VOL_WIDTH // 2))
    pool = pool_matrix()
    pools = (jnp.asarray(pool, BF), jnp.asarray(pool.T, BF))
    parts = [one_sample(volumes[s], cotangent[s], weights, masks, pools) for s in range(samples)]
    acts, inputs, firsts, seconds = zip(*parts)
    second_total = lax.psum(sum(seconds[1:], seconds[0]), ("sample", "space"))
    first_total = lax.psum(sum(firsts[1:], firsts[0]), ("sample", "space"))
    first_wgrad, first_bgrad = unpacked(first_total * scale, CH_MID)
    second_wgrad, second_bgrad = unpacked(second_total * scale, CH_OUT)
    return (
        jnp.stack(acts),
        jnp.stack(inputs),
        first_wgrad,
        first_bgrad,
        second_wgrad,
        second_bgrad,
    )


def solution(mesh):
    split = P("sample", None, "space", None)
    return jax.shard_map(
        per_device,
        mesh=mesh,
        in_specs=(split, P(), P(), P(), P(), split),
        out_specs=(split, split, P(), P(), P(), P()),
        check_vma=False,
    )
```

profile of v0, /device:TPU:1, one launch (start us, length us, event | category | flops | bytes accessed | tf_op | source)
XLA Modules:
  0.0 246.0 jit_solution(6288090244234804037)
XLA Ops:
  7.2 1.8 copy.64
  9.1 4.5 %collective-permute-start = (bf16[32,1024]{1,0:T(8,128)(2,1)S(1)}, bf16[32,1024]{1,0:T(8,128)(2,1)S(1)}, u32[]{:S(2)}, u32[]{:S(2)}) collective-permute-start(bf16[32,1024]{1,0:T(8,128)(2,1)S(1)} %get-tuple-element.23), channel_id=1, source_target_pairs={{0,1},{1,2},{2,3},{4,5},{5,6},{6,7},{8,9},{9,10},{10,11},{12,13},{... | collective-permute-start | bytes 196616 | tf_op jit(solution)/shard_map/ppermute | solution.py:207
  13.6 1.9 collective-permute-start.1
  16.6 3.6 %fusion.7.weight = bf16[256,6912]{1,0:T(8,128)(2,1)} fusion(bf16[64,3456]{1,0:T(8,128)(2,1)S(1)} %bitcast.50), kind=kLoop, calls=%fused_computation.13 | loop fusion | flops 35389440 | bytes 3981312 | tf_op jit(solution)/shard_map/concatenate | solution.py:42
  20.8 1.1 fusion.28.weight
  21.8 1.1 fusion.25.weight
  23.2 0.8 reshape_tile.8.bias
  24.6 17.3 %shard_map.145 = (bf16[512,256]{1,0:T(8,128)(2,1)}, bf16[1024,1024]{1,0:T(8,128)(2,1)}, bf16[5184,1024]{1,0:T(8,128)(2,1)}) custom-call(bf16[32,1024]{1,0:T(8,128)(2,1)} %copy-done.9, bf16[512,1024]{1,0:T(8,128)(2,1)} %bitcast.52, bf16[32,1024]{1,0:T(8,128)(2,1)} %copy-done.10, bf16[256,1728]{1,0:T(8,128)(2,1)} %fusion.25.weight, ...), custom_call_target="tpu_custom_call" | custom-call | flops 7247757312 | bytes 2491392 | tf_op jit(solution)/shard_map/pallas_call | solution.py:192
  41.9 0.8 fusion.33
  42.8 3.6 %collective-permute-start.2 = (bf16[64,256]{1,0:T(8,128)(2,1)S(1)}, bf16[64,256]{1,0:T(8,128)(2,1)S(1)}, u32[]{:S(2)}, u32[]{:S(2)}) collective-permute-start(bf16[64,256]{1,0:T(8,128)(2,1)S(1)} %get-tuple-element.29), channel_id=1, source_target_pairs={{0,1},{1,2},{2,3},{4,5},{5,6},{6,7},{8,9},{9,10},{10,11},{12,13},{... | collective-permute-start | bytes 98312 | tf_op jit(solution)/shard_map/ppermute | solution.py:207
  46.4 1.9 collective-permute-start.3
  48.3 1.2 fusion.23.weight
  49.6 0.9 copy.44
  50.5 0.8 copy.45.bias
  52.2 6.9 %shard_map.146 = (bf16[1024,256]{1,0:T(8,128)(2,1)}, bf16[1024,256]{1,0:T(8,128)(2,1)}, bf16[5760,256]{1,0:T(8,128)(2,1)}) custom-call(bf16[64,256]{1,0:T(8,128)(2,1)} %copy-done.13, bf16[512,256]{1,0:T(8,128)(2,1)} %get-tuple-element.12.x, bf16[64,256]{1,0:T(8,128)(2,1)} %copy-done.14, bf16[256,2304]{1,0:T(8,128)(2,1)} %fusion.23.weight, ...), custom_call_target="tpu_custom_call" | custom-call | flops 1811939328 | bytes 2106368 | tf_op jit(solution)/shard_map/pallas_call | solution.py:192
  59.1 0.9 fusion.32
  60.0 3.3 %collective-permute-start.4 = (bf16[128,256]{1,0:T(8,128)(2,1)S(1)}, bf16[128,256]{1,0:T(8,128)(2,1)S(1)}, u32[]{:S(2)}, u32[]{:S(2)}) collective-permute-start(bf16[128,256]{1,0:T(8,128)(2,1)S(1)} %get-tuple-element.27), channel_id=1, source_target_pairs={{0,1},{1,2},{2,3},{4,5},{5,6},{6,7},{8,9},{9,10},{10,11},{12,13},{... | collective-permute-start | bytes 196616 | tf_op jit(solution)/shard_map/ppermute | solution.py:207
  63.3 1.9 collective-permute-start.5
  65.3 6.5 %shard_map.150 = f32[592,384]{1,0:T(8,128)} custom-call(bf16[1024,256]{1,0:T(8,128)(2,1)} %get-tuple-element.14.x.grad, bf16[5760,256]{1,0:T(8,128)(2,1)} %get-tuple-element.17.col), custom_call_target="tpu_custom_call" | custom-call | flops 3623878656 | bytes 3473408 | tf_op jit(solution)/shard_map/pallas_call | solution.py:192
  71.8 1.1 copy.62
  73.5 9.4 %shard_map.147.x.grad = bf16[1024,1024]{1,0:T(8,128)(2,1)} custom-call(bf16[128,256]{1,0:T(8,128)(2,1)} %copy-done.11, bf16[1024,256]{1,0:T(8,128)(2,1)} %get-tuple-element.14.x.grad, bf16[128,256]{1,0:T(8,128)(2,1)} %copy-done.12, bf16[256,6912]{1,0:T(8,128)(2,1)} %fusion.7.weight, bf16[144,256]{1,0:T(8,128)(2,1)} %constant.15.clone.mask, ...), custom_call_target="tpu_custom_call" | custom-call | flops 3623878656 | bytes 6496256 | tf_op jit(solution)/shard_map/pallas_call | solution.py:192
  82.9 1.0 fusion.30
  83.9 3.6 %collective-permute-start.6 = (bf16[64,1024]{1,0:T(8,128)(2,1)S(1)}, bf16[64,1024]{1,0:T(8,128)(2,1)S(1)}, u32[]{:S(2)}, u32[]{:S(2)}) collective-permute-start(bf16[64,1024]{1,0:T(8,128)(2,1)S(1)} %get-tuple-element.21), channel_id=1, source_target_pairs={{0,1},{1,2},{2,3},{4,5},{5,6},{6,7},{8,9},{9,10},{10,11},{12,13},{... | collective-permute-start | bytes 393224 | tf_op jit(solution)/shard_map/ppermute | solution.py:207
  87.6 2.1 collective-permute-start.7
  89.7 11.8 %shard_map.149 = f32[304,192]{1,0:T(8,128)} custom-call(bf16[1024,1024]{1,0:T(8,128)(2,1)} %shard_map.147.x.grad, bf16[5184,1024]{1,0:T(8,128)(2,1)} %get-tuple-element.16.col), custom_call_target="tpu_custom_call" | custom-call | flops 7247757312 | bytes 12713984 | tf_op jit(solution)/shard_map/pallas_call | solution.py:192
  102.2 0.7 copy-done.8
  102.8 16.5 %shard_map.148 = bf16[512,1024]{1,0:T(8,128)(2,1)} custom-call(bf16[64,1024]{1,0:T(8,128)(2,1)} %copy-done.7, bf16[1024,1024]{1,0:T(8,128)(2,1)} %shard_map.147.x.grad, bf16[64,1024]{1,0:T(8,128)(2,1)} %copy-done.8, bf16[128,3456]{1,0:T(8,128)(2,1)} %fusion.28.weight, bf16[144,1024]{1,0:T(8,128)(2,1)} %constant.14.clone.mask), custom_call_target="tpu_custom_call" | custom-call | flops 10871635968 | bytes 3538944 | tf_op jit(solution)/shard_map/pallas_call | solution.py:192
  119.4 2.8 %copy.61 = bf16[16,32,1024]{2,0,1:T(8,128)(2,1)} copy(bf16[16,32,1024]{2,1,0:T(8,128)(2,1)} %bitcast.55) | data formatting | bytes 2097152 | tf_op jit(solution)/shard_map/reshape | solution.py:283
  122.1 111.7 %all-reduce.17.cloned.1.call-done = (f32[304,192]{1,0:T(8,128)}, f32[592,384]{1,0:T(8,128)}) async-done(((f32[304,192]{1,0:T(8,128)}, f32[592,384]{1,0:T(8,128)}), (f32[304,192]{1,0:T(8,128)}, f32[592,384]{1,0:T(8,128)})) %all-reduce.17.cloned.1.call-update) | async-done | bytes 1142800 | tf_op jit(solution)/shard_map/psum | solution.py:314
  233.8 1.3 broadcast_multiply_fusion
  236.7 1.2 copy.54
  238.3 0.9 reshape.61
  (62 shorter events, 6.6 us)
Async XLA Ops:
  7.2 8.4 %copy-start = (bf16[128,1728]{0,1:T(8,128)(2,1)S(1)}, bf16[128,1728]{0,1:T(8,128)(2,1)}, u32[]{:S(2)}) copy-start(bf16[128,1728]{0,1:T(8,128)(2,1)} %param.13) | copy-start | bytes 1327108
  7.2 226.6 %all-reduce.17.cloned.1.call-start = ((), (), s32[]{:S(2)}) async-start(), calls=%async_computation | async-start | bytes 2441216 | tf_op jit(solution)/shard_map/psum | solution.py:314
  9.1 11.2 %copy-start.1 = (bf16[1,32,16,1024]{3,1,2,0:T(8,128)(2,1)}, bf16[1,32,16,1024]{3,1,2,0:T(8,128)(2,1)S(1)}, u32[]{:S(2)}) copy-start(bf16[1,32,16,1024]{3,1,2,0:T(8,128)(2,1)S(1)} %copy.64) | copy-start | bytes 3145732
  9.1 14.9 %collective-permute-start = (bf16[32,1024]{1,0:T(8,128)(2,1)S(1)}, bf16[32,1024]{1,0:T(8,128)(2,1)S(1)}, u32[]{:S(2)}, u32[]{:S(2)}) collective-permute-start(bf16[32,1024]{1,0:T(8,128)(2,1)S(1)} %get-tuple-element.23), channel_id=1, source_target_pairs={{0,1},{1,2},{2,3},{4,5},{5,6},{6,7},{8,9},{9,10},{10,11},{12,13},{... | collective-permute-start | bytes 196616 | tf_op jit(solution)/shard_map/ppermute | solution.py:207
  13.6 10.4 %collective-permute-start.1 = (bf16[32,1024]{1,0:T(8,128)(2,1)S(1)}, bf16[32,1024]{1,0:T(8,128)(2,1)S(1)}, u32[]{:S(2)}, u32[]{:S(2)}) collective-permute-start(bf16[32,1024]{1,0:T(8,128)(2,1)S(1)} %get-tuple-element.22), channel_id=1, source_target_pairs={{1,0},{2,1},{3,2},{5,4},{6,5},{7,6},{9,8},{10,9},{11,10},{13,12},{... | collective-permute-start | bytes 196616 | tf_op jit(solution)/shard_map/ppermute | solution.py:208
  16.6 3.6 %copy-start.4 = (bf16[64,864]{1,0:T(8,128)(2,1)S(1)}, bf16[64,864]{1,0:T(8,128)(2,1)}, u32[]{:S(2)}) copy-start(bf16[64,864]{1,0:T(8,128)(2,1)} %param.11) | copy-start | bytes 331780
  20.4 2.7 %copy-start.6 = (f32[64]{0:T(128)S(1)}, f32[64]{0:T(128)}, u32[]{:S(2)}) copy-start(f32[64]{0:T(128)} %param.12) | copy-start | bytes 772
  24.0 0.6 copy-start.9
  24.0 0.6 copy-start.10
  41.9 7.6 %copy-start.2 = (bf16[1,128,8,256]{3,2,1,0:T(8,128)(2,1)S(1)}, bf16[1,128,8,256]{3,2,1,0:T(8,128)(2,1)}, u32[]{:S(2)}) copy-start(bf16[1,128,8,256]{3,2,1,0:T(8,128)(2,1)} %param.15) | copy-start | bytes 1572868
  41.9 8.5 %copy-start.15 = (f32[128]{0:T(128)S(1)}, f32[128]{0:T(128)}, u32[]{:S(2)}) copy-start(f32[128]{0:T(128)} %param.14) | copy-start | bytes 1540
  42.8 8.5 %collective-permute-start.2 = (bf16[64,256]{1,0:T(8,128)(2,1)S(1)}, bf16[64,256]{1,0:T(8,128)(2,1)S(1)}, u32[]{:S(2)}, u32[]{:S(2)}) collective-permute-start(bf16[64,256]{1,0:T(8,128)(2,1)S(1)} %get-tuple-element.29), channel_id=1, source_target_pairs={{0,1},{1,2},{2,3},{4,5},{5,6},{6,7},{8,9},{9,10},{10,11},{12,13},{... | collective-permute-start | bytes 98312 | tf_op jit(solution)/shard_map/ppermute | solution.py:207
  46.4 5.2 %collective-permute-start.3 = (bf16[64,256]{1,0:T(8,128)(2,1)S(1)}, bf16[64,256]{1,0:T(8,128)(2,1)S(1)}, u32[]{:S(2)}, u32[]{:S(2)}) collective-permute-start(bf16[64,256]{1,0:T(8,128)(2,1)S(1)} %get-tuple-element.28), channel_id=1, source_target_pairs={{1,0},{2,1},{3,2},{5,4},{6,5},{7,6},{9,8},{10,9},{11,10},{13,12},{... | collective-permute-start | bytes 98312 | tf_op jit(solution)/shard_map/ppermute | solution.py:208
  51.3 0.6 copy-start.13
  51.6 0.6 copy-start.14
  60.0 12.9 %collective-permute-start.4 = (bf16[128,256]{1,0:T(8,128)(2,1)S(1)}, bf16[128,256]{1,0:T(8,128)(2,1)S(1)}, u32[]{:S(2)}, u32[]{:S(2)}) collective-permute-start(bf16[128,256]{1,0:T(8,128)(2,1)S(1)} %get-tuple-element.27), channel_id=1, source_target_pairs={{0,1},{1,2},{2,3},{4,5},{5,6},{6,7},{8,9},{9,10},{10,11},{12,13},{... | collective-permute-start | bytes 196616 | tf_op jit(solution)/shard_map/ppermute | solution.py:207
  63.3 9.6 %collective-permute-start.5 = (bf16[128,256]{1,0:T(8,128)(2,1)S(1)}, bf16[128,256]{1,0:T(8,128)(2,1)S(1)}, u32[]{:S(2)}, u32[]{:S(2)}) collective-permute-start(bf16[128,256]{1,0:T(8,128)(2,1)S(1)} %get-tuple-element.26), channel_id=1, source_target_pairs={{1,0},{2,1},{3,2},{5,4},{6,5},{7,6},{9,8},{10,9},{11,10},{13,12},{... | collective-permute-start | bytes 196616 | tf_op jit(solution)/shard_map/ppermute | solution.py:208
  65.2 6.6 %copy-start.3 = (bf16[1024,256]{1,0:T(8,128)(2,1)S(1)}, bf16[1024,256]{1,0:T(8,128)(2,1)}, u32[]{:S(2)}) copy-start(bf16[1024,256]{1,0:T(8,128)(2,1)} %get-tuple-element.13) | copy-start | bytes 1572868
  72.9 0.6 copy-start.11
  72.9 0.6 copy-start.12
  83.9 17.6 %collective-permute-start.6 = (bf16[64,1024]{1,0:T(8,128)(2,1)S(1)}, bf16[64,1024]{1,0:T(8,128)(2,1)S(1)}, u32[]{:S(2)}, u32[]{:S(2)}) collective-permute-start(bf16[64,1024]{1,0:T(8,128)(2,1)S(1)} %get-tuple-element.21), channel_id=1, source_target_pairs={{0,1},{1,2},{2,3},{4,5},{5,6},{6,7},{8,9},{9,10},{10,11},{12,13},{... | collective-permute-start | bytes 393224 | tf_op jit(solution)/shard_map/ppermute | solution.py:207
  87.6 14.0 %collective-permute-start.7 = (bf16[64,1024]{1,0:T(8,128)(2,1)S(1)}, bf16[64,1024]{1,0:T(8,128)(2,1)S(1)}, u32[]{:S(2)}, u32[]{:S(2)}) collective-permute-start(bf16[64,1024]{1,0:T(8,128)(2,1)S(1)} %get-tuple-element.20), channel_id=1, source_target_pairs={{1,0},{2,1},{3,2},{5,4},{6,5},{7,6},{9,8},{10,9},{11,10},{13,12},{... | collective-permute-start | bytes 393224 | tf_op jit(solution)/shard_map/ppermute | solution.py:208
  101.5 0.7 copy-start.7
  102.2 0.7 copy-start.8
  233.8 1.9 copy-start.5
Sparse Core Ops, SparseCore 0:
  101.6 132.1 all-reduce.16
where the time goes:
time: 247 us; the launch traced here: 246 us
  waiting for transfers between devices  112 us (45%)
  Pallas kernels  68.5 us (28%)
  starting transfers between devices  23 us (9%)
  local copies, waits for them, and re-layouts  19.9 us (8%)
  between operations  14.3 us (6%)
  other arithmetic  8.32 us (3%)
    psum x1, waiting for transfers between devices, per_device(): first_total = lax.psum(sum(firsts[1:], firsts[0]), ('sample', 'space'))  112 us
    pallas_call x6, Pallas kernels, call(): pl.pallas_call(kernel, out_shape=[jax.ShapeDtypeStruct(shape, dtype) for...  68.5 us
    ppermute x4, starting transfers between devices, halo(): before = lax.ppermute(x[x.shape[0] - rows:], 'space', up)  15.1 us
    ppermute x4, starting transfers between devices, halo(): after = lax.ppermute(x[:rows], 'space', down)  7.86 us
    concatenate x4, other arithmetic, banded(): jnp.concatenate([jnp.pad(weight, ((0, 0), (j * taps, (planes - 1 - j) * t...  7.01 us
    unnamed x36, local copies, waits for them, and re-layouts  5.62 us
  transfers between devices with their start and end apart: 9, of which 2 were waited for; matrix products, arithmetic and copies ran while one was open for 6% of the time, Pallas kernels for 14%

commit v1 on v0

--- a/solution.py
+++ b/solution.py
@@ -216,7 +216,52 @@
     return group
 
 
-def one_sample(volume, cot, weights, masks, pools):
+def all_devices():
+    return lax.axis_size("sample") * lax.axis_size("space")
+
+
+def swapped(x, step):
+    pairs = [(i, i ^ step) for i in range(all_devices())]
+    return lax.ppermute(x.astype(BF), ("sample", "space"), pairs).astype(F32)
+
+
+def rounded(x):
+    return lax.reduce_precision(x, 8, 7)
+
+
+def doubled(total, step):
+    if step >= all_devices():
+        return total
+    mine = rounded(total)
+    return mine + swapped(mine, step)
+
+
+def is_upper():
+    return lax.axis_index("space") % 2 == 1
+
+
+def halved(total):
+    rows = total.shape[0] // 2
+    low, high = rounded(total[:rows]), rounded(total[rows:])
+    upper = is_upper()
+    return jnp.where(upper, high, low) + swapped(jnp.where(upper, low, high), 1)
+
+
+def joined(part):
+    mine = rounded(part)
+    other = swapped(mine, 1)
+    upper = is_upper()
+    return jnp.concatenate([jnp.where(upper, other, mine), jnp.where(upper, mine, other)])
+
+
+def finished(part, step, last):
+    while step < all_devices():
+        part = doubled(part, step)
+        step *= 2
+    return last(part)
+
+
+def one_sample(volume, cot, weights, masks, pools, alone):
     planes, cells = volume.shape[1:]
     half, small = planes // 2, cells // 4
     first_w, first_b, second_w, second_b, spread_w, input_w = weights
@@ -257,6 +302,8 @@
         2 * work,
         grad, small_col,
     )
+    if alone:
+        second_total = halved(second_total)
     (first_grad,) = call(
         spread_kernel,
         [((planes * CH_MID, cells), BF)],
@@ -265,13 +312,21 @@
         before, grad, after, spread_w, small_mask, pools[1], slope,
     )
     before, after = halo(first_grad, CH_MID)
+    local = first_grad
+    if alone:
+        local, second_total = lax.optimization_barrier((local, second_total))
+        second_total = doubled(second_total, 2)
     (first_total,) = call(
         functools.partial(weight_kernel, CH_MID),
         [((9 * CH_IN + 16, 3 * CH_MID), F32)],
         [(((planes + 4) * CH_MID, cells), BF)],
         4 * work,
-        first_grad, col,
-    )
+        local, col,
+    )
+    if alone:
+        before, second_total = lax.optimization_barrier((before, second_total))
+        second_total = doubled(second_total, 4)
+        first_total = doubled(first_total, 1)
     (input_grad,) = call(
         input_kernel,
         [((planes * CH_IN, cells), BF)],
@@ -308,10 +363,18 @@
     masks = (tap_masks(VOL_HEIGHT, VOL_WIDTH), tap_masks(VOL_HEIGHT // 2, VOL_WIDTH // 2))
     pool = pool_matrix()
     pools = (jnp.asarray(pool, BF), jnp.asarray(pool.T, BF))
-    parts = [one_sample(volumes[s], cotangent[s], weights, masks, pools) for s in range(samples)]
+    count = all_devices()
+    alone = samples == 1 and count & (count - 1) == 0 and lax.axis_size("space") % 2 == 0
+    parts = [
+        one_sample(volumes[s], cotangent[s], weights, masks, pools, alone) for s in range(samples)
+    ]
     acts, inputs, firsts, seconds = zip(*parts)
-    second_total = lax.psum(sum(seconds[1:], seconds[0]), ("sample", "space"))
-    first_total = lax.psum(sum(firsts[1:], firsts[0]), ("sample", "space"))
+    if alone:
+        second_total = finished(seconds[0], 8, joined)
+        first_total = finished(firsts[0], 2, lambda part: part)
+    else:
+        second_total = lax.psum(sum(seconds[1:], seconds[0]), ("sample", "space"))
+        first_total = lax.psum(sum(firsts[1:], firsts[0]), ("sample", "space"))
     first_wgrad, first_bgrad = unpacked(first_total * scale, CH_MID)
     second_wgrad, second_bgrad = unpacked(second_total * scale, CH_OUT)
     return (

time: 247 us -> 162 us (0.66)
  waiting for transfers between devices: 112 us -> 27.5 us
  between operations: 14.3 us -> 1.04 us
  starting transfers between devices: 23 us -> 33.5 us
  other arithmetic: 8.32 us -> 11.3 us
    psum x1 -> x0, waiting for transfers between devices: 112 us -> none  [per_device(): first_total = lax.psum(sum(firsts[1:], firsts[0]), ('sample', 'space'))]
    ppermute x0 -> x11, waiting for transfers between devices: none -> 25.8 us  [swapped(): return lax.ppermute(x.astype(BF), ('sample', 'space'), pairs).astype(F32)]
    ppermute x0 -> x11, starting transfers between devices: none -> 11.9 us  [swapped(): return lax.ppermute(x.astype(BF), ('sample', 'space'), pairs).astype(F32)]
    convert_element_type x0 -> x11, other arithmetic: none -> 3.91 us  [swapped(): return lax.ppermute(x.astype(BF), ('sample', 'space'), pairs).astype(F32)]
    unnamed x36 -> x38, local copies, waits for them, and re-layouts: 5.62 us -> 4.99 us
  transfers between devices with their start and end apart: 9 -> 19, of which waited for: 2 -> 7; matrix products, arithmetic and copies ran while one was open for 6% -> 14% of each run, Pallas kernels for 14% -> 23%
where the time goes in v1:
time: 162 us; the launch traced here: 161 us
  Pallas kernels  68.4 us (42%)
  starting transfers between devices  33.5 us (21%)
  waiting for transfers between devices  27.5 us (17%)
  local copies, waits for them, and re-layouts  19.2 us (12%)
  other arithmetic  11.3 us (7%)
    pallas_call x6, Pallas kernels, call(): pl.pallas_call(kernel, out_shape=[jax.ShapeDtypeStruct(shape, dtype) for...  68.4 us
    ppermute x11, waiting for transfers between devices, swapped(): return lax.ppermute(x.astype(BF), ('sample', 'space'), pairs).astype(F32)  25.8 us
    ppermute x4, starting transfers between devices, halo(): before = lax.ppermute(x[x.shape[0] - rows:], 'space', up)  13.8 us
    ppermute x11, starting transfers between devices, swapped(): return lax.ppermute(x.astype(BF), ('sample', 'space'), pairs).astype(F32)  11.9 us
    ppermute x4, starting transfers between devices, halo(): after = lax.ppermute(x[:rows], 'space', down)  7.89 us
    concatenate x4, other arithmetic, banded(): jnp.concatenate([jnp.pad(weight, ((0, 0), (j * taps, (planes - 1 - j) * t...  7.08 us
    unnamed x38, local copies, waits for them, and re-layouts  4.99 us
    convert_element_type x11, other arithmetic, swapped(): return lax.ppermute(x.astype(BF), ('sample', 'space'), pairs).astype(F32)  3.91 us
  transfers between devices with their start and end apart: 19, of which 7 were waited for; matrix products, arithmetic and copies ran while one was open for 14% of the time, Pallas kernels for 23%

profile of v1, /device:TPU:1, one launch (start us, length us, event | category | flops | bytes accessed | tf_op | source)
XLA Modules:
  0.0 161.1 jit_solution(15251936481226810342)
XLA Ops:
  0.6 1.9 %copy.64 = bf16[1,32,16,1024]{3,1,2,0:T(8,128)(2,1)S(1)} copy(bf16[1,32,16,1024]{3,2,1,0:T(8,128)(2,1)} %param.10) | data formatting | bytes 2097152 | tf_op args[0]
  2.5 4.5 %collective-permute-start = (bf16[32,1024]{1,0:T(8,128)(2,1)S(1)}, bf16[32,1024]{1,0:T(8,128)(2,1)S(1)}, u32[]{:S(2)}, u32[]{:S(2)}) collective-permute-start(bf16[32,1024]{1,0:T(8,128)(2,1)S(1)} %get-tuple-element.33), channel_id=1, source_target_pairs={{0,1},{1,2},{2,3},{4,5},{5,6},{6,7},{8,9},{9,10},{10,11},{12,13},{... | collective-permute-start | bytes 196616 | tf_op jit(solution)/shard_map/ppermute | solution.py:207
  7.0 1.9 %collective-permute-start.1 = (bf16[32,1024]{1,0:T(8,128)(2,1)S(1)}, bf16[32,1024]{1,0:T(8,128)(2,1)S(1)}, u32[]{:S(2)}, u32[]{:S(2)}) collective-permute-start(bf16[32,1024]{1,0:T(8,128)(2,1)S(1)} %get-tuple-element.32), channel_id=1, source_target_pairs={{1,0},{2,1},{3,2},{5,4},{6,5},{7,6},{9,8},{10,9},{11,10},{13,12},{... | collective-permute-start | bytes 196616 | tf_op jit(solution)/shard_map/ppermute | solution.py:208
  10.0 3.7 %fusion.7.weight = bf16[256,6912]{1,0:T(8,128)(2,1)} fusion(bf16[64,3456]{1,0:T(8,128)(2,1)S(1)} %bitcast.50), kind=kLoop, calls=%fused_computation.13 | loop fusion | flops 35389440 | bytes 3981312 | tf_op jit(solution)/shard_map/concatenate | solution.py:42
  18.1 17.3 %shard_map.145 = (bf16[512,256]{1,0:T(8,128)(2,1)}, bf16[1024,1024]{1,0:T(8,128)(2,1)}, bf16[5184,1024]{1,0:T(8,128)(2,1)}) custom-call(bf16[32,1024]{1,0:T(8,128)(2,1)} %copy-done.10, bf16[512,1024]{1,0:T(8,128)(2,1)} %bitcast.52, bf16[32,1024]{1,0:T(8,128)(2,1)} %copy-done.11, bf16[256,1728]{1,0:T(8,128)(2,1)} %fusion.25.weight, ...), custom_call_target="tpu_custom_call" | custom-call | flops 7247757312 | bytes 2491392 | tf_op jit(solution)/shard_map/pallas_call | solution.py:192
  36.2 3.6 %collective-permute-start.2 = (bf16[64,256]{1,0:T(8,128)(2,1)S(1)}, bf16[64,256]{1,0:T(8,128)(2,1)S(1)}, u32[]{:S(2)}, u32[]{:S(2)}) collective-permute-start(bf16[64,256]{1,0:T(8,128)(2,1)S(1)} %get-tuple-element.41), channel_id=1, source_target_pairs={{0,1},{1,2},{2,3},{4,5},{5,6},{6,7},{8,9},{9,10},{10,11},{12,13},{... | collective-permute-start | bytes 98312 | tf_op jit(solution)/shard_map/ppermute | solution.py:207
  39.9 1.9 %collective-permute-start.3 = (bf16[64,256]{1,0:T(8,128)(2,1)S(1)}, bf16[64,256]{1,0:T(8,128)(2,1)S(1)}, u32[]{:S(2)}, u32[]{:S(2)}) collective-permute-start(bf16[64,256]{1,0:T(8,128)(2,1)S(1)} %get-tuple-element.40), channel_id=1, source_target_pairs={{1,0},{2,1},{3,2},{5,4},{6,5},{7,6},{9,8},{10,9},{11,10},{13,12},{... | collective-permute-start | bytes 98312 | tf_op jit(solution)/shard_map/ppermute | solution.py:208
  41.8 1.2 fusion.23.weight
  45.7 6.9 %shard_map.146 = (bf16[1024,256]{1,0:T(8,128)(2,1)}, bf16[1024,256]{1,0:T(8,128)(2,1)}, bf16[5760,256]{1,0:T(8,128)(2,1)}) custom-call(bf16[64,256]{1,0:T(8,128)(2,1)} %copy-done.14, bf16[512,256]{1,0:T(8,128)(2,1)} %get-tuple-element.16.x, bf16[64,256]{1,0:T(8,128)(2,1)} %copy-done.15, bf16[256,2304]{1,0:T(8,128)(2,1)} %fusion.23.weight, ...), custom_call_target="tpu_custom_call" | custom-call | flops 1811939328 | bytes 2106368 | tf_op jit(solution)/shard_map/pallas_call | solution.py:192
  53.5 6.5 %shard_map.148 = f32[592,384]{1,0:T(8,128)} custom-call(bf16[1024,256]{1,0:T(8,128)(2,1)} %get-tuple-element.18.x.grad, bf16[5760,256]{1,0:T(8,128)(2,1)} %get-tuple-element.20.col), custom_call_target="tpu_custom_call" | custom-call | flops 3623878656 | bytes 3473408 | tf_op jit(solution)/shard_map/pallas_call | solution.py:192
  60.0 3.3 %collective-permute-start.4 = (bf16[128,256]{1,0:T(8,128)(2,1)S(1)}, bf16[128,256]{1,0:T(8,128)(2,1)S(1)}, u32[]{:S(2)}, u32[]{:S(2)}) collective-permute-start(bf16[128,256]{1,0:T(8,128)(2,1)S(1)} %get-tuple-element.39), channel_id=1, source_target_pairs={{0,1},{1,2},{2,3},{4,5},{5,6},{6,7},{8,9},{9,10},{10,11},{12,13},{... | collective-permute-start | bytes 196616 | tf_op jit(solution)/shard_map/ppermute | solution.py:207
  63.3 1.9 %collective-permute-start.5 = (bf16[128,256]{1,0:T(8,128)(2,1)S(1)}, bf16[128,256]{1,0:T(8,128)(2,1)S(1)}, u32[]{:S(2)}, u32[]{:S(2)}) collective-permute-start(bf16[128,256]{1,0:T(8,128)(2,1)S(1)} %get-tuple-element.38), channel_id=1, source_target_pairs={{1,0},{2,1},{3,2},{5,4},{6,5},{7,6},{9,8},{10,9},{11,10},{13,12},{... | collective-permute-start | bytes 196616 | tf_op jit(solution)/shard_map/ppermute | solution.py:208
  65.2 1.2 select_convert_fusion
  67.6 1.3 collective-permute-done.5.after
  69.5 9.4 %shard_map.147.x.grad = bf16[1024,1024]{1,0:T(8,128)(2,1)} custom-call(bf16[128,256]{1,0:T(8,128)(2,1)} %copy-done.12, bf16[1024,256]{1,0:T(8,128)(2,1)} %get-tuple-element.18.x.grad, bf16[128,256]{1,0:T(8,128)(2,1)} %copy-done.13, bf16[256,6912]{1,0:T(8,128)(2,1)} %fusion.7.weight, bf16[144,256]{1,0:T(8,128)(2,1)} %constant.35.clone.mask, ...), custom_call_target="tpu_custom_call" | custom-call | flops 3623878656 | bytes 6496256 | tf_op jit(solution)/shard_map/pallas_call | solution.py:192
  79.9 2.4 %collective-permute-start.6 = (bf16[64,1024]{1,0:T(8,128)(2,1)S(1)}, bf16[64,1024]{1,0:T(8,128)(2,1)S(1)}, u32[]{:S(2)}, u32[]{:S(2)}) collective-permute-start(bf16[64,1024]{1,0:T(8,128)(2,1)S(1)} %get-tuple-element.31), channel_id=1, source_target_pairs={{0,1},{1,2},{2,3},{4,5},{5,6},{6,7},{8,9},{9,10},{10,11},{12,13},{... | collective-permute-start | bytes 393224 | tf_op jit(solution)/shard_map/ppermute | solution.py:207
  82.3 2.1 %collective-permute-start.9 = (bf16[64,1024]{1,0:T(8,128)(2,1)S(1)}, bf16[64,1024]{1,0:T(8,128)(2,1)S(1)}, u32[]{:S(2)}, u32[]{:S(2)}) collective-permute-start(bf16[64,1024]{1,0:T(8,128)(2,1)S(1)} %get-tuple-element.30), channel_id=1, source_target_pairs={{1,0},{2,1},{3,2},{5,4},{6,5},{7,6},{9,8},{10,9},{11,10},{13,12},{... | collective-permute-start | bytes 393224 | tf_op jit(solution)/shard_map/ppermute | solution.py:208
  84.6 11.8 %shard_map.150 = f32[304,192]{1,0:T(8,128)} custom-call(bf16[1024,1024]{1,0:T(8,128)(2,1)} %shard_map.147.x.grad, bf16[5184,1024]{1,0:T(8,128)(2,1)} %get-tuple-element.24.col), custom_call_target="tpu_custom_call" | custom-call | flops 7247757312 | bytes 12713984 | tf_op jit(solution)/shard_map/pallas_call | solution.py:192
  97.6 1.9 %collective-permute-start.8 = (bf16[296,384]{1,0:T(8,128)(2,1)S(1)}, bf16[296,384]{1,0:T(8,128)(2,1)S(1)}, u32[]{:S(2)}, u32[]{:S(2)}) collective-permute-start(bf16[296,384]{1,0:T(8,128)(2,1)S(1)} %reduce-precision_convert_fusion.1), channel_id=1, source_target_pairs={{0,2},{1,3},{2,0},{3,1},{4,6},{5,7},{6,4},{7,5},{8,10},{9,11},{10,... | collective-permute-start | bytes 681992 | tf_op jit(solution)/shard_map/ppermute | solution.py:225
  101.4 3.6 %collective-permute-done.8 = bf16[296,384]{1,0:T(8,128)(2,1)S(1)} collective-permute-done((bf16[296,384]{1,0:T(8,128)(2,1)S(1)}, bf16[296,384]{1,0:T(8,128)(2,1)S(1)}, u32[]{:S(2)}, u32[]{:S(2)}) %collective-permute-start.8) | collective-permute-done | bytes 227360 | tf_op jit(solution)/shard_map/ppermute | solution.py:225
  105.1 1.3 collective-permute-start.15
  106.4 1.9 %collective-permute-done.11 = bf16[304,192]{1,0:T(8,128)(2,1)S(1)} collective-permute-done((bf16[304,192]{1,0:T(8,128)(2,1)S(1)}, bf16[304,192]{1,0:T(8,128)(2,1)S(1)}, u32[]{:S(2)}, u32[]{:S(2)}) %collective-permute-start.11) | collective-permute-done | bytes 116768 | tf_op jit(solution)/shard_map/ppermute | solution.py:225
  108.4 1.3 collective-permute-start.12
  110.4 16.5 %shard_map.149 = bf16[512,1024]{1,0:T(8,128)(2,1)} custom-call(bf16[64,1024]{1,0:T(8,128)(2,1)} %copy-done.8, bf16[1024,1024]{1,0:T(8,128)(2,1)} %shard_map.147.x.grad, bf16[64,1024]{1,0:T(8,128)(2,1)} %copy-done.9, bf16[128,3456]{1,0:T(8,128)(2,1)} %fusion.28.weight, bf16[144,1024]{1,0:T(8,128)(2,1)} %constant.34.clone.mask), custom_call_target="tpu_custom_call" | custom-call | flops 10871635968 | bytes 3538944 | tf_op jit(solution)/shard_map/pallas_call | solution.py:192
  126.9 2.8 %copy.61 = bf16[16,32,1024]{2,0,1:T(8,128)(2,1)} copy(bf16[16,32,1024]{2,1,0:T(8,128)(2,1)} %bitcast.55) | data formatting | bytes 2097152 | tf_op jit(solution)/shard_map/reshape | solution.py:338
  129.8 1.4 collective-permute-start.13
  131.5 2.5 %collective-permute-done.13 = bf16[304,192]{1,0:T(8,128)(2,1)S(1)} collective-permute-done((bf16[304,192]{1,0:T(8,128)(2,1)S(1)}, bf16[304,192]{1,0:T(8,128)(2,1)S(1)}, u32[]{:S(2)}, u32[]{:S(2)}) %collective-permute-start.13) | collective-permute-done | bytes 116768 | tf_op jit(solution)/shard_map/ppermute | solution.py:225
  134.0 2.4 %collective-permute-start.14 = (bf16[304,192]{1,0:T(8,128)(2,1)S(1)}, bf16[304,192]{1,0:T(8,128)(2,1)S(1)}, u32[]{:S(2)}, u32[]{:S(2)}) collective-permute-start(bf16[304,192]{1,0:T(8,128)(2,1)S(1)} %fusion.32), channel_id=1, source_target_pairs={{0,16},{1,17},{2,18},{3,19},{4,20},{5,21},{6,22},{7,23},{8,24},{9,... | collective-permute-start | bytes 350216 | tf_op jit(solution)/shard_map/ppermute | solution.py:225
  136.4 4.3 %collective-permute-done.16 = bf16[296,384]{1,0:T(8,128)(2,1)S(1)} collective-permute-done((bf16[296,384]{1,0:T(8,128)(2,1)S(1)}, bf16[296,384]{1,0:T(8,128)(2,1)S(1)}, u32[]{:S(2)}, u32[]{:S(2)}) %collective-permute-start.16) | collective-permute-done | bytes 227360 | tf_op jit(solution)/shard_map/ppermute | solution.py:225
  140.8 1.3 collective-permute-start.17
  142.4 13.6 %collective-permute-done.17 = bf16[296,384]{1,0:T(8,128)(2,1)S(1)} collective-permute-done((bf16[296,384]{1,0:T(8,128)(2,1)S(1)}, bf16[296,384]{1,0:T(8,128)(2,1)S(1)}, u32[]{:S(2)}, u32[]{:S(2)}) %collective-permute-start.17) | collective-permute-done | bytes 227360 | tf_op jit(solution)/shard_map/ppermute | solution.py:225
  159.8 1.2 copy.54
  (97 shorter events, 21.3 us)
Async XLA Ops:
  0.6 8.3 %copy-start.2 = (bf16[128,1728]{0,1:T(8,128)(2,1)S(1)}, bf16[128,1728]{0,1:T(8,128)(2,1)}, u32[]{:S(2)}) copy-start(bf16[128,1728]{0,1:T(8,128)(2,1)} %param.13) | copy-start | bytes 1327108
  2.5 11.2 %copy-start.3 = (bf16[1,32,16,1024]{3,1,2,0:T(8,128)(2,1)}, bf16[1,32,16,1024]{3,1,2,0:T(8,128)(2,1)S(1)}, u32[]{:S(2)}) copy-start(bf16[1,32,16,1024]{3,1,2,0:T(8,128)(2,1)S(1)} %copy.64) | copy-start | bytes 3145732
  2.5 15.0 %collective-permute-start = (bf16[32,1024]{1,0:T(8,128)(2,1)S(1)}, bf16[32,1024]{1,0:T(8,128)(2,1)S(1)}, u32[]{:S(2)}, u32[]{:S(2)}) collective-permute-start(bf16[32,1024]{1,0:T(8,128)(2,1)S(1)} %get-tuple-element.33), channel_id=1, source_target_pairs={{0,1},{1,2},{2,3},{4,5},{5,6},{6,7},{8,9},{9,10},{10,11},{12,13},{... | collective-permute-start | bytes 196616 | tf_op jit(solution)/shard_map/ppermute | solution.py:207
  7.0 10.4 %collective-permute-start.1 = (bf16[32,1024]{1,0:T(8,128)(2,1)S(1)}, bf16[32,1024]{1,0:T(8,128)(2,1)S(1)}, u32[]{:S(2)}, u32[]{:S(2)}) collective-permute-start(bf16[32,1024]{1,0:T(8,128)(2,1)S(1)} %get-tuple-element.32), channel_id=1, source_target_pairs={{1,0},{2,1},{3,2},{5,4},{6,5},{7,6},{9,8},{10,9},{11,10},{13,12},{... | collective-permute-start | bytes 196616 | tf_op jit(solution)/shard_map/ppermute | solution.py:208
  10.0 3.7 %copy-start.6 = (bf16[64,864]{1,0:T(8,128)(2,1)S(1)}, bf16[64,864]{1,0:T(8,128)(2,1)}, u32[]{:S(2)}) copy-start(bf16[64,864]{1,0:T(8,128)(2,1)} %param.11) | copy-start | bytes 331780
  13.9 2.8 %copy-start.7 = (f32[64]{0:T(128)S(1)}, f32[64]{0:T(128)}, u32[]{:S(2)}) copy-start(f32[64]{0:T(128)} %param.12) | copy-start | bytes 772
  17.5 0.6 copy-start.10
  35.4 7.6 %copy-start.4 = (bf16[1,128,8,256]{3,2,1,0:T(8,128)(2,1)S(1)}, bf16[1,128,8,256]{3,2,1,0:T(8,128)(2,1)}, u32[]{:S(2)}) copy-start(bf16[1,128,8,256]{3,2,1,0:T(8,128)(2,1)} %param.15) | copy-start | bytes 1572868
  35.4 8.5 %copy-start.16 = (f32[128]{0:T(128)S(1)}, f32[128]{0:T(128)}, u32[]{:S(2)}) copy-start(f32[128]{0:T(128)} %param.14) | copy-start | bytes 1540
  36.2 8.5 %collective-permute-start.2 = (bf16[64,256]{1,0:T(8,128)(2,1)S(1)}, bf16[64,256]{1,0:T(8,128)(2,1)S(1)}, u32[]{:S(2)}, u32[]{:S(2)}) collective-permute-start(bf16[64,256]{1,0:T(8,128)(2,1)S(1)} %get-tuple-element.41), channel_id=1, source_target_pairs={{0,1},{1,2},{2,3},{4,5},{5,6},{6,7},{8,9},{9,10},{10,11},{12,13},{... | collective-permute-start | bytes 98312 | tf_op jit(solution)/shard_map/ppermute | solution.py:207
  39.9 5.2 %collective-permute-start.3 = (bf16[64,256]{1,0:T(8,128)(2,1)S(1)}, bf16[64,256]{1,0:T(8,128)(2,1)S(1)}, u32[]{:S(2)}, u32[]{:S(2)}) collective-permute-start(bf16[64,256]{1,0:T(8,128)(2,1)S(1)} %get-tuple-element.40), channel_id=1, source_target_pairs={{1,0},{2,1},{3,2},{5,4},{6,5},{7,6},{9,8},{10,9},{11,10},{13,12},{... | collective-permute-start | bytes 98312 | tf_op jit(solution)/shard_map/ppermute | solution.py:208
  53.5 13.0 %copy-start.5 = (bf16[1024,256]{1,0:T(8,128)(2,1)S(1)}, bf16[1024,256]{1,0:T(8,128)(2,1)}, u32[]{:S(2)}) copy-start(bf16[1024,256]{1,0:T(8,128)(2,1)} %get-tuple-element.17) | copy-start | bytes 1572868
  60.0 7.6 %collective-permute-start.4 = (bf16[128,256]{1,0:T(8,128)(2,1)S(1)}, bf16[128,256]{1,0:T(8,128)(2,1)S(1)}, u32[]{:S(2)}, u32[]{:S(2)}) collective-permute-start(bf16[128,256]{1,0:T(8,128)(2,1)S(1)} %get-tuple-element.39), channel_id=1, source_target_pairs={{0,1},{1,2},{2,3},{4,5},{5,6},{6,7},{8,9},{9,10},{10,11},{12,13},{... | collective-permute-start | bytes 196616 | tf_op jit(solution)/shard_map/ppermute | solution.py:207
  63.3 5.6 %collective-permute-start.5 = (bf16[128,256]{1,0:T(8,128)(2,1)S(1)}, bf16[128,256]{1,0:T(8,128)(2,1)S(1)}, u32[]{:S(2)}, u32[]{:S(2)}) collective-permute-start(bf16[128,256]{1,0:T(8,128)(2,1)S(1)} %get-tuple-element.38), channel_id=1, source_target_pairs={{1,0},{2,1},{3,2},{5,4},{6,5},{7,6},{9,8},{10,9},{11,10},{13,12},{... | collective-permute-start | bytes 196616 | tf_op jit(solution)/shard_map/ppermute | solution.py:208
  66.4 18.0 %collective-permute-start.7 = (bf16[296,384]{1,0:T(8,128)(2,1)S(1)}, bf16[296,384]{1,0:T(8,128)(2,1)S(1)}, u32[]{:S(2)}, u32[]{:S(2)}) collective-permute-start(bf16[296,384]{1,0:T(8,128)(2,1)S(1)} %select_convert_fusion), channel_id=1, source_target_pairs={{0,1},{1,0},{2,3},{3,2},{4,5},{5,4},{6,7},{7,6},{8,9},{9,8},{10,11... | collective-permute-start | bytes 681992 | tf_op jit(solution)/shard_map/ppermute | solution.py:225
  67.6 1.3 copy-start.12
  69.5 15.0 %copy-start.1 = (f32[592,384]{1,0:T(8,128)S(1)}, f32[592,384]{1,0:T(8,128)}, u32[]{:S(2)}) copy-start(f32[592,384]{1,0:T(8,128)} %shard_map.148) | copy-start | bytes 2727940
  79.9 25.1 %collective-permute-start.6 = (bf16[64,1024]{1,0:T(8,128)(2,1)S(1)}, bf16[64,1024]{1,0:T(8,128)(2,1)S(1)}, u32[]{:S(2)}, u32[]{:S(2)}) collective-permute-start(bf16[64,1024]{1,0:T(8,128)(2,1)S(1)} %get-tuple-element.31), channel_id=1, source_target_pairs={{0,1},{1,2},{2,3},{4,5},{5,6},{6,7},{8,9},{9,10},{10,11},{12,13},{... | collective-permute-start | bytes 393224 | tf_op jit(solution)/shard_map/ppermute | solution.py:207
  82.3 27.4 %collective-permute-start.9 = (bf16[64,1024]{1,0:T(8,128)(2,1)S(1)}, bf16[64,1024]{1,0:T(8,128)(2,1)S(1)}, u32[]{:S(2)}, u32[]{:S(2)}) collective-permute-start(bf16[64,1024]{1,0:T(8,128)(2,1)S(1)} %get-tuple-element.30), channel_id=1, source_target_pairs={{1,0},{2,1},{3,2},{5,4},{6,5},{7,6},{9,8},{10,9},{11,10},{13,12},{... | collective-permute-start | bytes 393224 | tf_op jit(solution)/shard_map/ppermute | solution.py:208
  96.4 11.9 %copy-start = (f32[304,192]{1,0:T(8,128)S(1)}, f32[304,192]{1,0:T(8,128)}, u32[]{:S(2)}) copy-start(f32[304,192]{1,0:T(8,128)} %shard_map.150) | copy-start | bytes 700420
  97.5 2.0 %collective-permute-start.10 = (bf16[304,192]{1,0:T(8,128)(2,1)S(1)}, bf16[304,192]{1,0:T(8,128)(2,1)S(1)}, u32[]{:S(2)}, u32[]{:S(2)}) collective-permute-start(bf16[304,192]{1,0:T(8,128)(2,1)S(1)} %reduce-precision_convert_fusion.2), channel_id=1, source_target_pairs={{0,1},{1,0},{2,3},{3,2},{4,5},{5,4},{6,7},{7,6},{8,9},{9,8},{10,11... | collective-permute-start | bytes 350216 | tf_op jit(solution)/shard_map/ppermute | solution.py:225
  97.6 7.4 %collective-permute-start.8 = (bf16[296,384]{1,0:T(8,128)(2,1)S(1)}, bf16[296,384]{1,0:T(8,128)(2,1)S(1)}, u32[]{:S(2)}, u32[]{:S(2)}) collective-permute-start(bf16[296,384]{1,0:T(8,128)(2,1)S(1)} %reduce-precision_convert_fusion.1), channel_id=1, source_target_pairs={{0,2},{1,3},{2,0},{3,1},{4,6},{5,7},{6,4},{7,5},{8,10},{9,11},{10,... | collective-permute-start | bytes 681992 | tf_op jit(solution)/shard_map/ppermute | solution.py:225
  100.4 7.9 %collective-permute-start.11 = (bf16[304,192]{1,0:T(8,128)(2,1)S(1)}, bf16[304,192]{1,0:T(8,128)(2,1)S(1)}, u32[]{:S(2)}, u32[]{:S(2)}) collective-permute-start(bf16[304,192]{1,0:T(8,128)(2,1)S(1)} %fusion.34), channel_id=1, source_target_pairs={{0,2},{1,3},{2,0},{3,1},{4,6},{5,7},{6,4},{7,5},{8,10},{9,11},{10,... | collective-permute-start | bytes 350216 | tf_op jit(solution)/shard_map/ppermute | solution.py:225
  105.1 4.7 %copy-start.8 = (bf16[64,1024]{1,0:T(8,128)(2,1)}, bf16[64,1024]{1,0:T(8,128)(2,1)S(1)}, u32[]{:S(2)}) copy-start(bf16[64,1024]{1,0:T(8,128)(2,1)S(1)} %collective-permute-done.6.before) | copy-start | bytes 393220
  105.1 26.1 %collective-permute-start.15 = (bf16[296,384]{1,0:T(8,128)(2,1)S(1)}, bf16[296,384]{1,0:T(8,128)(2,1)S(1)}, u32[]{:S(2)}, u32[]{:S(2)}) collective-permute-start(bf16[296,384]{1,0:T(8,128)(2,1)S(1)} %reduce-precision_convert_fusion), channel_id=1, source_target_pairs={{0,4},{1,5},{2,6},{3,7},{4,0},{5,1},{6,2},{7,3},{8,12},{9,13},{10,... | collective-permute-start | bytes 681992 | tf_op jit(solution)/shard_map/ppermute | solution.py:225
  108.4 21.3 %collective-permute-start.12 = (bf16[304,192]{1,0:T(8,128)(2,1)S(1)}, bf16[304,192]{1,0:T(8,128)(2,1)S(1)}, u32[]{:S(2)}, u32[]{:S(2)}) collective-permute-start(bf16[304,192]{1,0:T(8,128)(2,1)S(1)} %fusion.31), channel_id=1, source_target_pairs={{0,4},{1,5},{2,6},{3,7},{4,0},{5,1},{6,2},{7,3},{8,12},{9,13},{10,... | collective-permute-start | bytes 350216 | tf_op jit(solution)/shard_map/ppermute | solution.py:225
  109.7 0.7 copy-start.9
  129.8 4.1 %collective-permute-start.13 = (bf16[304,192]{1,0:T(8,128)(2,1)S(1)}, bf16[304,192]{1,0:T(8,128)(2,1)S(1)}, u32[]{:S(2)}, u32[]{:S(2)}) collective-permute-start(bf16[304,192]{1,0:T(8,128)(2,1)S(1)} %get-tuple-element.28), channel_id=1, source_target_pairs={{0,8},{1,9},{2,10},{3,11},{4,12},{5,13},{6,14},{7,15},{8,0},{9,1},... | collective-permute-start | bytes 350216 | tf_op jit(solution)/shard_map/ppermute | solution.py:225
  131.2 9.4 %collective-permute-start.16 = (bf16[296,384]{1,0:T(8,128)(2,1)S(1)}, bf16[296,384]{1,0:T(8,128)(2,1)S(1)}, u32[]{:S(2)}, u32[]{:S(2)}) collective-permute-start(bf16[296,384]{1,0:T(8,128)(2,1)S(1)} %fusion.33), channel_id=1, source_target_pairs={{0,8},{1,9},{2,10},{3,11},{4,12},{5,13},{6,14},{7,15},{8,0},{9,1},... | collective-permute-start | bytes 681992 | tf_op jit(solution)/shard_map/ppermute | solution.py:225
  134.0 8.1 %collective-permute-start.14 = (bf16[304,192]{1,0:T(8,128)(2,1)S(1)}, bf16[304,192]{1,0:T(8,128)(2,1)S(1)}, u32[]{:S(2)}, u32[]{:S(2)}) collective-permute-start(bf16[304,192]{1,0:T(8,128)(2,1)S(1)} %fusion.32), channel_id=1, source_target_pairs={{0,16},{1,17},{2,18},{3,19},{4,20},{5,21},{6,22},{7,23},{8,24},{9,... | collective-permute-start | bytes 350216 | tf_op jit(solution)/shard_map/ppermute | solution.py:225
  140.8 15.1 %collective-permute-start.17 = (bf16[296,384]{1,0:T(8,128)(2,1)S(1)}, bf16[296,384]{1,0:T(8,128)(2,1)S(1)}, u32[]{:S(2)}, u32[]{:S(2)}) collective-permute-start(bf16[296,384]{1,0:T(8,128)(2,1)S(1)} %fusion.30), channel_id=1, source_target_pairs={{0,16},{1,17},{2,18},{3,19},{4,20},{5,21},{6,22},{7,23},{8,24},{9,... | collective-permute-start | bytes 681992 | tf_op jit(solution)/shard_map/ppermute | solution.py:225
  156.1 2.6 %collective-permute-start.18 = (bf16[296,384]{1,0:T(8,128)(2,1)S(1)}, bf16[296,384]{1,0:T(8,128)(2,1)S(1)}, u32[]{:S(2)}, u32[]{:S(2)}) collective-permute-start(bf16[296,384]{1,0:T(8,128)(2,1)S(1)} %get-tuple-element.26), channel_id=1, source_target_pairs={{0,1},{1,0},{2,3},{3,2},{4,5},{5,4},{6,7},{7,6},{8,9},{9,8},{10,11... | collective-permute-start | bytes 681992 | tf_op jit(solution)/shard_map/ppermute | solution.py:225
  (4 other events, 2.5 us)

commit v2 on v1

--- a/solution.py
+++ b/solution.py
@@ -254,8 +254,8 @@
     return jnp.concatenate([jnp.where(upper, other, mine), jnp.where(upper, mine, other)])
 
 
-def finished(part, step, last):
-    while step < all_devices():
+def finished(part, step, end, last):
+    while step < end:
         part = doubled(part, step)
         step *= 2
     return last(part)
@@ -315,7 +315,7 @@
     local = first_grad
     if alone:
         local, second_total = lax.optimization_barrier((local, second_total))
-        second_total = doubled(second_total, 2)
+        second_total = doubled(second_total, all_devices() // 4)
     (first_total,) = call(
         functools.partial(weight_kernel, CH_MID),
         [((9 * CH_IN + 16, 3 * CH_MID), F32)],
@@ -324,9 +324,11 @@
         local, col,
     )
     if alone:
-        before, second_total = lax.optimization_barrier((before, second_total))
-        second_total = doubled(second_total, 4)
-        first_total = doubled(first_total, 1)
+        before, first_total, second_total = lax.optimization_barrier(
+            (before, first_total, second_total)
+        )
+        second_total = doubled(second_total, all_devices() // 2)
+        first_total = doubled(first_total, all_devices() // 2)
     (input_grad,) = call(
         input_kernel,
         [((planes * CH_IN, cells), BF)],
@@ -334,6 +336,10 @@
         6 * work,
         before, first_grad, after, input_w, big_mask,
     )
+    if alone:
+        input_grad, first_total, second_total = lax.optimization_barrier(
+            (input_grad, first_total, second_total)
+        )
     act = act.reshape(half, CH_OUT, small).transpose(1, 0, 2)
     input_grad = input_grad.reshape(planes, CH_IN, cells).transpose(1, 0, 2)
     return act, input_grad, first_total, second_total
@@ -364,14 +370,14 @@
     pool = pool_matrix()
     pools = (jnp.asarray(pool, BF), jnp.asarray(pool.T, BF))
     count = all_devices()
-    alone = samples == 1 and count & (count - 1) == 0 and lax.axis_size("space") % 2 == 0
+    alone = samples == 1 and count >= 8 and count & (count - 1) == 0 and lax.axis_size("space") % 2 == 0
     parts = [
         one_sample(volumes[s], cotangent[s], weights, masks, pools, alone) for s in range(samples)
     ]
     acts, inputs, firsts, seconds = zip(*parts)
     if alone:
-        second_total = finished(seconds[0], 8, joined)
-        first_total = finished(firsts[0], 2, lambda part: part)
+        second_total = finished(seconds[0], 2, count // 4, joined)
+        first_total = finished(firsts[0], 1, count // 2, lambda part: part)
     else:
         second_total = lax.psum(sum(seconds[1:], seconds[0]), ("sample", "space"))
         first_total = lax.psum(sum(firsts[1:], firsts[0]), ("sample", "space"))

time: 162 us -> 144 us (0.89)
  waiting for transfers between devices: 27.5 us -> 13 us
  other arithmetic: 11.3 us -> 9.37 us
    ppermute x11, waiting for transfers between devices: 25.8 us -> 10.3 us  [swapped(): return lax.ppermute(x.astype(BF), ('sample', 'space'), pairs).astype(F32)]
    convert_element_type x11, other arithmetic: 3.91 us -> 1.73 us  [swapped(): return lax.ppermute(x.astype(BF), ('sample', 'space'), pairs).astype(F32)]
    unnamed x38 -> x40, local copies, waits for them, and re-layouts: 4.99 us -> 5.81 us
  transfers between devices with their start and end apart: 19 -> 19, of which waited for: 7 -> 5; matrix products, arithmetic and copies ran while one was open for 14% -> 13% of each run, Pallas kernels for 23% -> 26%
where the time goes in v2:
time: 144 us
  Pallas kernels  68.4 us (48%)
  starting transfers between devices  32.8 us (23%)
  local copies, waits for them, and re-layouts  18.8 us (13%)
  waiting for transfers between devices  13 us (9%)
  other arithmetic  9.37 us (7%)
    pallas_call x6, Pallas kernels, call(): pl.pallas_call(kernel, out_shape=[jax.ShapeDtypeStruct(shape, dtype) for...  68.4 us
    ppermute x4, starting transfers between devices, halo(): before = lax.ppermute(x[x.shape[0] - rows:], 'space', up)  13.3 us
    ppermute x11, starting transfers between devices, swapped(): return lax.ppermute(x.astype(BF), ('sample', 'space'), pairs).astype(F32)  11.1 us
    ppermute x11, waiting for transfers between devices, swapped(): return lax.ppermute(x.astype(BF), ('sample', 'space'), pairs).astype(F32)  10.3 us
    ppermute x4, starting transfers between devices, halo(): after = lax.ppermute(x[:rows], 'space', down)  8.35 us
    concatenate x4, other arithmetic, banded(): jnp.concatenate([jnp.pad(weight, ((0, 0), (j * taps, (planes - 1 - j) * t...  7.03 us
    unnamed x40, local copies, waits for them, and re-layouts  5.81 us
  transfers between devices with their start and end apart: 19, of which 5 were waited for; matrix products, arithmetic and copies ran while one was open for 13% of the time, Pallas kernels for 26%

profile of v2, /device:TPU:1, one launch (start us, length us, event | category | flops | bytes accessed | tf_op | source)
XLA Modules:
  0.0 143.5 jit_solution(11975941450581324085)
XLA Ops:
  0.6 1.9 %copy.64 = bf16[1,32,16,1024]{3,1,2,0:T(8,128)(2,1)S(1)} copy(bf16[1,32,16,1024]{3,2,1,0:T(8,128)(2,1)} %param.10) | data formatting | bytes 2097152 | tf_op args[0]
  2.5 4.5 %collective-permute-start = (bf16[32,1024]{1,0:T(8,128)(2,1)S(1)}, bf16[32,1024]{1,0:T(8,128)(2,1)S(1)}, u32[]{:S(2)}, u32[]{:S(2)}) collective-permute-start(bf16[32,1024]{1,0:T(8,128)(2,1)S(1)} %get-tuple-element.39), channel_id=1, source_target_pairs={{0,1},{1,2},{2,3},{4,5},{5,6},{6,7},{8,9},{9,10},{10,11},{12,13},{... | collective-permute-start | bytes 196616 | tf_op jit(solution)/shard_map/ppermute | solution.py:207
  7.0 1.9 %collective-permute-start.1 = (bf16[32,1024]{1,0:T(8,128)(2,1)S(1)}, bf16[32,1024]{1,0:T(8,128)(2,1)S(1)}, u32[]{:S(2)}, u32[]{:S(2)}) collective-permute-start(bf16[32,1024]{1,0:T(8,128)(2,1)S(1)} %get-tuple-element.38), channel_id=1, source_target_pairs={{1,0},{2,1},{3,2},{5,4},{6,5},{7,6},{9,8},{10,9},{11,10},{13,12},{... | collective-permute-start | bytes 196616 | tf_op jit(solution)/shard_map/ppermute | solution.py:208
  10.0 3.6 %fusion.7.weight = bf16[256,6912]{1,0:T(8,128)(2,1)} fusion(bf16[64,3456]{1,0:T(8,128)(2,1)S(1)} %bitcast.50), kind=kLoop, calls=%fused_computation.13 | loop fusion | flops 35389440 | bytes 3981312 | tf_op jit(solution)/shard_map/concatenate | solution.py:42
  15.3 1.1 fusion.25.weight
  18.1 17.3 %shard_map.145 = (bf16[512,256]{1,0:T(8,128)(2,1)}, bf16[1024,1024]{1,0:T(8,128)(2,1)}, bf16[5184,1024]{1,0:T(8,128)(2,1)}) custom-call(bf16[32,1024]{1,0:T(8,128)(2,1)} %copy-done.11, bf16[512,1024]{1,0:T(8,128)(2,1)} %bitcast.52, bf16[32,1024]{1,0:T(8,128)(2,1)} %copy-done.12, bf16[256,1728]{1,0:T(8,128)(2,1)} %fusion.25.weight, ...), custom_call_target="tpu_custom_call" | custom-call | flops 7247757312 | bytes 2491392 | tf_op jit(solution)/shard_map/pallas_call | solution.py:192
  36.2 3.6 %collective-permute-start.2 = (bf16[64,256]{1,0:T(8,128)(2,1)S(1)}, bf16[64,256]{1,0:T(8,128)(2,1)S(1)}, u32[]{:S(2)}, u32[]{:S(2)}) collective-permute-start(bf16[64,256]{1,0:T(8,128)(2,1)S(1)} %get-tuple-element.45), channel_id=1, source_target_pairs={{0,1},{1,2},{2,3},{4,5},{5,6},{6,7},{8,9},{9,10},{10,11},{12,13},{... | collective-permute-start | bytes 98312 | tf_op jit(solution)/shard_map/ppermute | solution.py:207
  39.8 1.9 %collective-permute-start.3 = (bf16[64,256]{1,0:T(8,128)(2,1)S(1)}, bf16[64,256]{1,0:T(8,128)(2,1)S(1)}, u32[]{:S(2)}, u32[]{:S(2)}) collective-permute-start(bf16[64,256]{1,0:T(8,128)(2,1)S(1)} %get-tuple-element.44), channel_id=1, source_target_pairs={{1,0},{2,1},{3,2},{5,4},{6,5},{7,6},{9,8},{10,9},{11,10},{13,12},{... | collective-permute-start | bytes 98312 | tf_op jit(solution)/shard_map/ppermute | solution.py:208
  41.7 1.2 fusion.23.weight
  45.7 6.9 %shard_map.146 = (bf16[1024,256]{1,0:T(8,128)(2,1)}, bf16[1024,256]{1,0:T(8,128)(2,1)}, bf16[5760,256]{1,0:T(8,128)(2,1)}) custom-call(bf16[64,256]{1,0:T(8,128)(2,1)} %copy-done.15, bf16[512,256]{1,0:T(8,128)(2,1)} %get-tuple-element.20.x, bf16[64,256]{1,0:T(8,128)(2,1)} %copy-done.16, bf16[256,2304]{1,0:T(8,128)(2,1)} %fusion.23.weight, ...), custom_call_target="tpu_custom_call" | custom-call | flops 1811939328 | bytes 2106368 | tf_op jit(solution)/shard_map/pallas_call | solution.py:192
  53.4 6.5 %shard_map.148 = f32[592,384]{1,0:T(8,128)} custom-call(bf16[1024,256]{1,0:T(8,128)(2,1)} %get-tuple-element.22.x.grad, bf16[5760,256]{1,0:T(8,128)(2,1)} %get-tuple-element.24.col), custom_call_target="tpu_custom_call" | custom-call | flops 3623878656 | bytes 3473408 | tf_op jit(solution)/shard_map/pallas_call | solution.py:192
  59.9 3.3 %collective-permute-start.4 = (bf16[128,256]{1,0:T(8,128)(2,1)S(1)}, bf16[128,256]{1,0:T(8,128)(2,1)S(1)}, u32[]{:S(2)}, u32[]{:S(2)}) collective-permute-start(bf16[128,256]{1,0:T(8,128)(2,1)S(1)} %get-tuple-element.43), channel_id=1, source_target_pairs={{0,1},{1,2},{2,3},{4,5},{5,6},{6,7},{8,9},{9,10},{10,11},{12,13},{... | collective-permute-start | bytes 196616 | tf_op jit(solution)/shard_map/ppermute | solution.py:207
  63.2 1.9 %collective-permute-start.5 = (bf16[128,256]{1,0:T(8,128)(2,1)S(1)}, bf16[128,256]{1,0:T(8,128)(2,1)S(1)}, u32[]{:S(2)}, u32[]{:S(2)}) collective-permute-start(bf16[128,256]{1,0:T(8,128)(2,1)S(1)} %get-tuple-element.42), channel_id=1, source_target_pairs={{1,0},{2,1},{3,2},{5,4},{6,5},{7,6},{9,8},{10,9},{11,10},{13,12},{... | collective-permute-start | bytes 196616 | tf_op jit(solution)/shard_map/ppermute | solution.py:208
  65.1 1.2 select_convert_fusion
  66.4 2.4 %collective-permute-done.5.after = bf16[128,256]{1,0:T(8,128)(2,1)S(1)} collective-permute-done((bf16[128,256]{1,0:T(8,128)(2,1)S(1)}, bf16[128,256]{1,0:T(8,128)(2,1)S(1)}, u32[]{:S(2)}, u32[]{:S(2)}) %collective-permute-start.5) | collective-permute-done | bytes 65568 | tf_op jit(solution)/shard_map/ppermute | solution.py:208
  69.4 9.4 %shard_map.147.grad.x = bf16[1024,1024]{1,0:T(8,128)(2,1)} custom-call(bf16[128,256]{1,0:T(8,128)(2,1)} %copy-done.13, bf16[1024,256]{1,0:T(8,128)(2,1)} %get-tuple-element.22.x.grad, bf16[128,256]{1,0:T(8,128)(2,1)} %copy-done.14, bf16[256,6912]{1,0:T(8,128)(2,1)} %fusion.7.weight, bf16[144,256]{1,0:T(8,128)(2,1)} %constant.35.clone.mask, ...), custom_call_target="tpu_custom_call" | custom-call | flops 3623878656 | bytes 6496256 | tf_op jit(solution)/shard_map/pallas_call | solution.py:192
  79.8 1.9 %collective-permute-start.6 = (bf16[64,1024]{1,0:T(8,128)(2,1)S(1)}, bf16[64,1024]{1,0:T(8,128)(2,1)S(1)}, u32[]{:S(2)}, u32[]{:S(2)}) collective-permute-start(bf16[64,1024]{1,0:T(8,128)(2,1)S(1)} %get-tuple-element.35), channel_id=1, source_target_pairs={{0,1},{1,2},{2,3},{4,5},{5,6},{6,7},{8,9},{9,10},{10,11},{12,13},{... | collective-permute-start | bytes 393224 | tf_op jit(solution)/shard_map/ppermute | solution.py:207
  81.8 2.6 %collective-permute-start.9 = (bf16[64,1024]{1,0:T(8,128)(2,1)S(1)}, bf16[64,1024]{1,0:T(8,128)(2,1)S(1)}, u32[]{:S(2)}, u32[]{:S(2)}) collective-permute-start(bf16[64,1024]{1,0:T(8,128)(2,1)S(1)} %get-tuple-element.34), channel_id=1, source_target_pairs={{1,0},{2,1},{3,2},{5,4},{6,5},{7,6},{9,8},{10,9},{11,10},{13,12},{... | collective-permute-start | bytes 393224 | tf_op jit(solution)/shard_map/ppermute | solution.py:208
  84.5 1.3 collective-permute-start.8
  85.8 11.8 %shard_map.149 = f32[304,192]{1,0:T(8,128)} custom-call(bf16[1024,1024]{1,0:T(8,128)(2,1)} %shard_map.147.grad.x, bf16[5184,1024]{1,0:T(8,128)(2,1)} %get-tuple-element.26.col), custom_call_target="tpu_custom_call" | custom-call | flops 7247757312 | bytes 12713984 | tf_op jit(solution)/shard_map/pallas_call | solution.py:192
  97.8 2.4 %collective-permute-start.11 = (bf16[296,384]{1,0:T(8,128)(2,1)S(1)}, bf16[296,384]{1,0:T(8,128)(2,1)S(1)}, u32[]{:S(2)}, u32[]{:S(2)}) collective-permute-start(bf16[296,384]{1,0:T(8,128)(2,1)S(1)} %reduce-precision_convert_fusion.1), channel_id=1, source_target_pairs={{0,16},{1,17},{2,18},{3,19},{4,20},{5,21},{6,22},{7,23},{8,24},{9,... | collective-permute-start | bytes 681992 | tf_op jit(solution)/shard_map/ppermute | solution.py:225
  101.7 16.5 %shard_map.150 = bf16[512,1024]{1,0:T(8,128)(2,1)} custom-call(bf16[64,1024]{1,0:T(8,128)(2,1)} %copy-done.9, bf16[1024,1024]{1,0:T(8,128)(2,1)} %shard_map.147.grad.x, bf16[64,1024]{1,0:T(8,128)(2,1)} %copy-done.10, bf16[128,3456]{1,0:T(8,128)(2,1)} %fusion.28.weight, bf16[144,1024]{1,0:T(8,128)(2,1)} %constant.34.clone.mask), custom_call_target="tpu_custom_call" | custom-call | flops 10871635968 | bytes 3538944 | tf_op jit(solution)/shard_map/pallas_call | solution.py:192
  119.2 1.1 copy.62
  120.4 1.2 collective-permute-start.13
  122.0 1.5 %copy.61 = bf16[16,32,1024]{2,0,1:T(8,128)(2,1)} copy(bf16[16,32,1024]{2,1,0:T(8,128)(2,1)S(1)} %bitcast.55) | data formatting | bytes 2097152 | tf_op jit(solution)/shard_map/reshape | solution.py:344
  123.6 2.4 %collective-permute-done.13 = bf16[304,192]{1,0:T(8,128)(2,1)S(1)} collective-permute-done((bf16[304,192]{1,0:T(8,128)(2,1)S(1)}, bf16[304,192]{1,0:T(8,128)(2,1)S(1)}, u32[]{:S(2)}, u32[]{:S(2)}) %collective-permute-start.13) | collective-permute-done | bytes 116768 | tf_op jit(solution)/shard_map/ppermute | solution.py:225
  126.0 1.3 collective-permute-start.14
  127.3 3.5 %collective-permute-done.16 = bf16[296,384]{1,0:T(8,128)(2,1)S(1)} collective-permute-done((bf16[296,384]{1,0:T(8,128)(2,1)S(1)}, bf16[296,384]{1,0:T(8,128)(2,1)S(1)}, u32[]{:S(2)}, u32[]{:S(2)}) %collective-permute-start.16) | collective-permute-done | bytes 227360 | tf_op jit(solution)/shard_map/ppermute | solution.py:225
  130.9 1.3 collective-permute-start.17
  132.5 4.5 %collective-permute-done.17 = bf16[296,384]{1,0:T(8,128)(2,1)S(1)} collective-permute-done((bf16[296,384]{1,0:T(8,128)(2,1)S(1)}, bf16[296,384]{1,0:T(8,128)(2,1)S(1)}, u32[]{:S(2)}, u32[]{:S(2)}) %collective-permute-start.17) | collective-permute-done | bytes 227360 | tf_op jit(solution)/shard_map/ppermute | solution.py:225
  137.1 2.0 %collective-permute-start.18 = (bf16[296,384]{1,0:T(8,128)(2,1)S(1)}, bf16[296,384]{1,0:T(8,128)(2,1)S(1)}, u32[]{:S(2)}, u32[]{:S(2)}) collective-permute-start(bf16[296,384]{1,0:T(8,128)(2,1)S(1)} %fusion.34), channel_id=1, source_target_pairs={{0,1},{1,0},{2,3},{3,2},{4,5},{5,4},{6,7},{7,6},{8,9},{9,8},{10,11... | collective-permute-start | bytes 681992 | tf_op jit(solution)/shard_map/ppermute | solution.py:225
  142.3 1.2 copy.54
  (101 shorter events, 17.3 us)
Async XLA Ops:
  0.6 8.3 %copy-start.1 = (bf16[128,1728]{0,1:T(8,128)(2,1)S(1)}, bf16[128,1728]{0,1:T(8,128)(2,1)}, u32[]{:S(2)}) copy-start(bf16[128,1728]{0,1:T(8,128)(2,1)} %param.13) | copy-start | bytes 1327108
  2.5 11.1 %copy-start.2 = (bf16[1,32,16,1024]{3,1,2,0:T(8,128)(2,1)}, bf16[1,32,16,1024]{3,1,2,0:T(8,128)(2,1)S(1)}, u32[]{:S(2)}) copy-start(bf16[1,32,16,1024]{3,1,2,0:T(8,128)(2,1)S(1)} %copy.64) | copy-start | bytes 3145732
  2.5 14.9 %collective-permute-start = (bf16[32,1024]{1,0:T(8,128)(2,1)S(1)}, bf16[32,1024]{1,0:T(8,128)(2,1)S(1)}, u32[]{:S(2)}, u32[]{:S(2)}) collective-permute-start(bf16[32,1024]{1,0:T(8,128)(2,1)S(1)} %get-tuple-element.39), channel_id=1, source_target_pairs={{0,1},{1,2},{2,3},{4,5},{5,6},{6,7},{8,9},{9,10},{10,11},{12,13},{... | collective-permute-start | bytes 196616 | tf_op jit(solution)/shard_map/ppermute | solution.py:207
  7.0 10.4 %collective-permute-start.1 = (bf16[32,1024]{1,0:T(8,128)(2,1)S(1)}, bf16[32,1024]{1,0:T(8,128)(2,1)S(1)}, u32[]{:S(2)}, u32[]{:S(2)}) collective-permute-start(bf16[32,1024]{1,0:T(8,128)(2,1)S(1)} %get-tuple-element.38), channel_id=1, source_target_pairs={{1,0},{2,1},{3,2},{5,4},{6,5},{7,6},{9,8},{10,9},{11,10},{13,12},{... | collective-permute-start | bytes 196616 | tf_op jit(solution)/shard_map/ppermute | solution.py:208
  10.0 3.6 %copy-start.7 = (bf16[64,864]{1,0:T(8,128)(2,1)S(1)}, bf16[64,864]{1,0:T(8,128)(2,1)}, u32[]{:S(2)}) copy-start(bf16[64,864]{1,0:T(8,128)(2,1)} %param.11) | copy-start | bytes 331780
  13.8 2.8 %copy-start.8 = (f32[64]{0:T(128)S(1)}, f32[64]{0:T(128)}, u32[]{:S(2)}) copy-start(f32[64]{0:T(128)} %param.12) | copy-start | bytes 772
  35.3 7.7 %copy-start.5 = (bf16[1,128,8,256]{3,2,1,0:T(8,128)(2,1)S(1)}, bf16[1,128,8,256]{3,2,1,0:T(8,128)(2,1)}, u32[]{:S(2)}) copy-start(bf16[1,128,8,256]{3,2,1,0:T(8,128)(2,1)} %param.15) | copy-start | bytes 1572868
  35.3 8.5 %copy-start.17 = (f32[128]{0:T(128)S(1)}, f32[128]{0:T(128)}, u32[]{:S(2)}) copy-start(f32[128]{0:T(128)} %param.14) | copy-start | bytes 1540
  36.2 8.5 %collective-permute-start.2 = (bf16[64,256]{1,0:T(8,128)(2,1)S(1)}, bf16[64,256]{1,0:T(8,128)(2,1)S(1)}, u32[]{:S(2)}, u32[]{:S(2)}) collective-permute-start(bf16[64,256]{1,0:T(8,128)(2,1)S(1)} %get-tuple-element.45), channel_id=1, source_target_pairs={{0,1},{1,2},{2,3},{4,5},{5,6},{6,7},{8,9},{9,10},{10,11},{12,13},{... | collective-permute-start | bytes 98312 | tf_op jit(solution)/shard_map/ppermute | solution.py:207
  39.8 5.2 %collective-permute-start.3 = (bf16[64,256]{1,0:T(8,128)(2,1)S(1)}, bf16[64,256]{1,0:T(8,128)(2,1)S(1)}, u32[]{:S(2)}, u32[]{:S(2)}) collective-permute-start(bf16[64,256]{1,0:T(8,128)(2,1)S(1)} %get-tuple-element.44), channel_id=1, source_target_pairs={{1,0},{2,1},{3,2},{5,4},{6,5},{7,6},{9,8},{10,9},{11,10},{13,12},{... | collective-permute-start | bytes 98312 | tf_op jit(solution)/shard_map/ppermute | solution.py:208
  59.9 6.5 %collective-permute-start.4 = (bf16[128,256]{1,0:T(8,128)(2,1)S(1)}, bf16[128,256]{1,0:T(8,128)(2,1)S(1)}, u32[]{:S(2)}, u32[]{:S(2)}) collective-permute-start(bf16[128,256]{1,0:T(8,128)(2,1)S(1)} %get-tuple-element.43), channel_id=1, source_target_pairs={{0,1},{1,2},{2,3},{4,5},{5,6},{6,7},{8,9},{9,10},{10,11},{12,13},{... | collective-permute-start | bytes 196616 | tf_op jit(solution)/shard_map/ppermute | solution.py:207
  63.2 5.6 %collective-permute-start.5 = (bf16[128,256]{1,0:T(8,128)(2,1)S(1)}, bf16[128,256]{1,0:T(8,128)(2,1)S(1)}, u32[]{:S(2)}, u32[]{:S(2)}) collective-permute-start(bf16[128,256]{1,0:T(8,128)(2,1)S(1)} %get-tuple-element.42), channel_id=1, source_target_pairs={{1,0},{2,1},{3,2},{5,4},{6,5},{7,6},{9,8},{10,9},{11,10},{13,12},{... | collective-permute-start | bytes 196616 | tf_op jit(solution)/shard_map/ppermute | solution.py:208
  66.3 18.0 %collective-permute-start.7 = (bf16[296,384]{1,0:T(8,128)(2,1)S(1)}, bf16[296,384]{1,0:T(8,128)(2,1)S(1)}, u32[]{:S(2)}, u32[]{:S(2)}) collective-permute-start(bf16[296,384]{1,0:T(8,128)(2,1)S(1)} %select_convert_fusion), channel_id=1, source_target_pairs={{0,1},{1,0},{2,3},{3,2},{4,5},{5,4},{6,7},{7,6},{8,9},{9,8},{10,11... | collective-permute-start | bytes 681992 | tf_op jit(solution)/shard_map/ppermute | solution.py:225
  66.4 2.4 %copy-start.13 = (bf16[128,256]{1,0:T(8,128)(2,1)}, bf16[128,256]{1,0:T(8,128)(2,1)S(1)}, u32[]{:S(2)}) copy-start(bf16[128,256]{1,0:T(8,128)(2,1)S(1)} %collective-permute-done.4.before) | copy-start | bytes 196612
  69.4 15.0 %copy-start = (f32[592,384]{1,0:T(8,128)S(1)}, f32[592,384]{1,0:T(8,128)}, u32[]{:S(2)}) copy-start(f32[592,384]{1,0:T(8,128)} %shard_map.148) | copy-start | bytes 2727940
  79.8 17.9 %collective-permute-start.6 = (bf16[64,1024]{1,0:T(8,128)(2,1)S(1)}, bf16[64,1024]{1,0:T(8,128)(2,1)S(1)}, u32[]{:S(2)}, u32[]{:S(2)}) collective-permute-start(bf16[64,1024]{1,0:T(8,128)(2,1)S(1)} %get-tuple-element.35), channel_id=1, source_target_pairs={{0,1},{1,2},{2,3},{4,5},{5,6},{6,7},{8,9},{9,10},{10,11},{12,13},{... | collective-permute-start | bytes 393224 | tf_op jit(solution)/shard_map/ppermute | solution.py:207
  81.8 19.3 %collective-permute-start.9 = (bf16[64,1024]{1,0:T(8,128)(2,1)S(1)}, bf16[64,1024]{1,0:T(8,128)(2,1)S(1)}, u32[]{:S(2)}, u32[]{:S(2)}) collective-permute-start(bf16[64,1024]{1,0:T(8,128)(2,1)S(1)} %get-tuple-element.34), channel_id=1, source_target_pairs={{1,0},{2,1},{3,2},{5,4},{6,5},{7,6},{9,8},{10,9},{11,10},{13,12},{... | collective-permute-start | bytes 393224 | tf_op jit(solution)/shard_map/ppermute | solution.py:208
  84.5 13.2 %collective-permute-start.8 = (bf16[296,384]{1,0:T(8,128)(2,1)S(1)}, bf16[296,384]{1,0:T(8,128)(2,1)S(1)}, u32[]{:S(2)}, u32[]{:S(2)}) collective-permute-start(bf16[296,384]{1,0:T(8,128)(2,1)S(1)} %reduce-precision_convert_fusion.2), channel_id=1, source_target_pairs={{0,8},{1,9},{2,10},{3,11},{4,12},{5,13},{6,14},{7,15},{8,0},{9,1},... | collective-permute-start | bytes 681992 | tf_op jit(solution)/shard_map/ppermute | solution.py:225
  97.7 2.5 %copy-start.3 = (f32[304,192]{1,0:T(8,128)S(1)}, f32[304,192]{1,0:T(8,128)}, u32[]{:S(2)}) copy-start(f32[304,192]{1,0:T(8,128)} %shard_map.149) | copy-start | bytes 700420
  97.7 3.3 %copy-start.9 = (bf16[64,1024]{1,0:T(8,128)(2,1)}, bf16[64,1024]{1,0:T(8,128)(2,1)S(1)}, u32[]{:S(2)}) copy-start(bf16[64,1024]{1,0:T(8,128)(2,1)S(1)} %collective-permute-done.6.before) | copy-start | bytes 393220
  97.8 20.5 %collective-permute-start.11 = (bf16[296,384]{1,0:T(8,128)(2,1)S(1)}, bf16[296,384]{1,0:T(8,128)(2,1)S(1)}, u32[]{:S(2)}, u32[]{:S(2)}) collective-permute-start(bf16[296,384]{1,0:T(8,128)(2,1)S(1)} %reduce-precision_convert_fusion.1), channel_id=1, source_target_pairs={{0,16},{1,17},{2,18},{3,19},{4,20},{5,21},{6,22},{7,23},{8,24},{9,... | collective-permute-start | bytes 681992 | tf_op jit(solution)/shard_map/ppermute | solution.py:225
  100.2 18.0 %collective-permute-start.10 = (bf16[304,192]{1,0:T(8,128)(2,1)S(1)}, bf16[304,192]{1,0:T(8,128)(2,1)S(1)}, u32[]{:S(2)}, u32[]{:S(2)}) collective-permute-start(bf16[304,192]{1,0:T(8,128)(2,1)S(1)} %reduce-precision_convert_fusion.4), channel_id=1, source_target_pairs={{0,16},{1,17},{2,18},{3,19},{4,20},{5,21},{6,22},{7,23},{8,24},{9,... | collective-permute-start | bytes 350216 | tf_op jit(solution)/shard_map/ppermute | solution.py:225
  101.0 0.7 copy-start.10
  118.2 1.0 copy-start.6
  118.3 3.8 %copy-start.4 = (bf16[512,1024]{1,0:T(8,128)(2,1)S(1)}, bf16[512,1024]{1,0:T(8,128)(2,1)}, u32[]{:S(2)}) copy-start(bf16[512,1024]{1,0:T(8,128)(2,1)} %shard_map.150) | copy-start | bytes 3145732
  118.4 2.0 %collective-permute-start.12 = (bf16[304,192]{1,0:T(8,128)(2,1)S(1)}, bf16[304,192]{1,0:T(8,128)(2,1)S(1)}, u32[]{:S(2)}, u32[]{:S(2)}) collective-permute-start(bf16[304,192]{1,0:T(8,128)(2,1)S(1)} %reduce-precision_convert_fusion.3), channel_id=1, source_target_pairs={{0,1},{1,0},{2,3},{3,2},{4,5},{5,4},{6,7},{7,6},{8,9},{9,8},{10,11... | collective-permute-start | bytes 350216 | tf_op jit(solution)/shard_map/ppermute | solution.py:225
  120.4 5.5 %collective-permute-start.13 = (bf16[304,192]{1,0:T(8,128)(2,1)S(1)}, bf16[304,192]{1,0:T(8,128)(2,1)S(1)}, u32[]{:S(2)}, u32[]{:S(2)}) collective-permute-start(bf16[304,192]{1,0:T(8,128)(2,1)S(1)} %fusion.33), channel_id=1, source_target_pairs={{0,2},{1,3},{2,0},{3,1},{4,6},{5,7},{6,4},{7,5},{8,10},{9,11},{10,... | collective-permute-start | bytes 350216 | tf_op jit(solution)/shard_map/ppermute | solution.py:225
  121.6 9.2 %collective-permute-start.16 = (bf16[296,384]{1,0:T(8,128)(2,1)S(1)}, bf16[296,384]{1,0:T(8,128)(2,1)S(1)}, u32[]{:S(2)}, u32[]{:S(2)}) collective-permute-start(bf16[296,384]{1,0:T(8,128)(2,1)S(1)} %reduce-precision_convert_fusion), channel_id=1, source_target_pairs={{0,2},{1,3},{2,0},{3,1},{4,6},{5,7},{6,4},{7,5},{8,10},{9,11},{10,... | collective-permute-start | bytes 681992 | tf_op jit(solution)/shard_map/ppermute | solution.py:225
  126.0 6.2 %collective-permute-start.14 = (bf16[304,192]{1,0:T(8,128)(2,1)S(1)}, bf16[304,192]{1,0:T(8,128)(2,1)S(1)}, u32[]{:S(2)}, u32[]{:S(2)}) collective-permute-start(bf16[304,192]{1,0:T(8,128)(2,1)S(1)} %fusion.31), channel_id=1, source_target_pairs={{0,4},{1,5},{2,6},{3,7},{4,0},{5,1},{6,2},{7,3},{8,12},{9,13},{10,... | collective-permute-start | bytes 350216 | tf_op jit(solution)/shard_map/ppermute | solution.py:225
  130.9 6.2 %collective-permute-start.17 = (bf16[296,384]{1,0:T(8,128)(2,1)S(1)}, bf16[296,384]{1,0:T(8,128)(2,1)S(1)}, u32[]{:S(2)}, u32[]{:S(2)}) collective-permute-start(bf16[296,384]{1,0:T(8,128)(2,1)S(1)} %fusion.30), channel_id=1, source_target_pairs={{0,4},{1,5},{2,6},{3,7},{4,0},{5,1},{6,2},{7,3},{8,12},{9,13},{10,... | collective-permute-start | bytes 681992 | tf_op jit(solution)/shard_map/ppermute | solution.py:225
  132.3 6.8 %collective-permute-start.15 = (bf16[304,192]{1,0:T(8,128)(2,1)S(1)}, bf16[304,192]{1,0:T(8,128)(2,1)S(1)}, u32[]{:S(2)}, u32[]{:S(2)}) collective-permute-start(bf16[304,192]{1,0:T(8,128)(2,1)S(1)} %fusion.32), channel_id=1, source_target_pairs={{0,8},{1,9},{2,10},{3,11},{4,12},{5,13},{6,14},{7,15},{8,0},{9,1},... | collective-permute-start | bytes 350216 | tf_op jit(solution)/shard_map/ppermute | solution.py:225
  137.1 3.9 %collective-permute-start.18 = (bf16[296,384]{1,0:T(8,128)(2,1)S(1)}, bf16[296,384]{1,0:T(8,128)(2,1)S(1)}, u32[]{:S(2)}, u32[]{:S(2)}) collective-permute-start(bf16[296,384]{1,0:T(8,128)(2,1)S(1)} %fusion.34), channel_id=1, source_target_pairs={{0,1},{1,0},{2,3},{3,2},{4,5},{5,4},{6,7},{7,6},{8,9},{9,8},{10,11... | collective-permute-start | bytes 681992 | tf_op jit(solution)/shard_map/ppermute | solution.py:225
  (5 other events, 3.1 us)
